TPU v7x, 32 devices: a whole 2x2x4 slice. The times are simulated.
32 devices in a mesh: row: 16 (over z, y, core), col: 2 (over x).
Axes of the slice: x: 2, y: 2, z: 4, core: 2. Of those that a mesh axis runs over, the one named last changes fastest.
Arguments:
- weight: float32 [8192, 4096], P('row', 'col'), may hold values from -0.0625 to 0.0625
- grad: bfloat16 [8192, 4096], P('row', 'col'), may hold values from -6 to 6
- left: bfloat16 [8192, 8192], P('row', 'col'), may hold values from -0.25 to 3, as said below
- right: bfloat16 [4096, 4096], P('row', 'col'), may hold values from -0.25 to 3, as said below
- tokens: bfloat16 [2048, 8192], P('row'), may hold values from -6 to 6
Outputs:
- new_weight: float32 [8192, 4096], P('row', 'col')
- output: bfloat16 [2048, 4096], P('row', 'col')
Inputs may be any that keep to these rules, and one draw needn't show every extreme that they name: left is symmetric. right is symmetric.
All inputs are finite; a program needn't handle non-finite values.
Results may differ from a plain program's by a relative error of at most 0.0056.
Values may be sent and summed in bfloat16 or wider, within the bound.
No kernel may reach another device: no remote copies, remote signals or barrier semaphores. Data moves between devices by JAX's collectives and lax.ppermute only.
A program may use at most 128 MiB of HBM per device.

v0:
```python
import jax
import jax.numpy as jnp
from jax import lax
from jax.sharding import PartitionSpec as P


def shards(weight, grad, left, right, tokens):
    left_panel = lax.all_gather(left, "col", axis=1, tiled=True)
    left_total = jnp.dot(
        left_panel,
        lax.all_gather(grad, "row", axis=0, tiled=True),
        preferred_element_type=jnp.float32,
    )
    left_grad = left_total.astype(jnp.bfloat16)
    right_panel = lax.all_gather(right, "row", axis=0, tiled=True)
    selected = right_panel
    precond = jnp.dot(
        lax.all_gather(left_grad, "col", axis=1, tiled=True),
        selected,
        preferred_element_type=jnp.float32,
    )
    new_weight = weight - 0.01 * precond
    narrow = new_weight.astype(jnp.bfloat16)
    spread = lax.all_to_all(tokens, "row", split_axis=1, concat_axis=0, tiled=True)
    selected = spread
    output = lax.psum_scatter(
        jnp.dot(selected, narrow, preferred_element_type=jnp.float32),
        "row",
        scatter_dimension=0,
        tiled=True,
    )
    return (new_weight, output.astype(jnp.bfloat16))


def solution(mesh):
    return jax.shard_map(
        shards,
        mesh=mesh,
        in_specs=(
            P("row", "col"),
            P("row", "col"),
            P("row", "col"),
            P("row", "col"),
            P("row", None),
        ),
        out_specs=(P("row", "col"), P("row", "col")),
        check_vma=False,
    )
```

profile of v0, /device:TPU:0, one launch (start us, length us, event | category | flops | bytes accessed | tf_op | source)
XLA Modules:
  0.0 719.3 jit_solution(8812150631302011817)
XLA Ops:
  7.2 0.0 all-gather.5.cloned.1.call-start
  7.2 0.7 all-gather.5.cloned.1.call-update
  7.9 0.0 all-gather.7.cloned.1.call-start
  7.9 0.7 all-gather.7.cloned.1.call-update
  8.6 0.0 all-gather.11.cloned.1.call-start
  8.7 0.7 all-gather.11.cloned.1.call-update
  9.4 0.0 copy-start
  9.4 0.0 all-gather.9.cloned.1.call-start
  9.4 106.8 %all-gather.5.cloned.1.call-done = bf16[512,8192]{1,0:T(8,128)(2,1)} async-done(((bf16[512,4096]{1,0:T(8,128)(2,1)}), bf16[512,8192]{1,0:T(8,128)(2,1)}) %all-gather.5.cloned.1.call-update) | async-done | bytes 8388624 | tf_op jit(solution)/shard_map/all_gather | solution.py:8
  116.3 169.7 %all-gather.7.cloned.1.call-done = bf16[8192,2048]{1,0:T(8,128)(2,1)} async-done(((bf16[512,2048]{1,0:T(8,128)(2,1)}), bf16[8192,2048]{1,0:T(8,128)(2,1)}) %all-gather.7.cloned.1.call-update) | async-done | bytes 33554448 | tf_op jit(solution)/shard_map/all_gather | solution.py:11
  286.0 24.6 %convolution_convert_fusion = bf16[512,2048]{1,0:T(8,128)(2,1)} fusion(bf16[512,8192]{1,0:T(8,128)(2,1)} %all-gather.5.cloned.1.call-done, bf16[8192,2048]{1,0:T(8,128)(2,1)} %all-gather.7.cloned.1.call-done), kind=kOutput, calls=%fused_computation.2 | convolution fusion | flops 17180917760 | bytes 44040192 | tf_op jit(solution)/shard_map/dot_general | solution.py:9
  310.5 0.0 all-gather.9.cloned.1.call-update
  310.6 0.0 reduce-scatter.2.cloned.1.call-start
  310.6 0.0 copy-done
  310.6 2.4 copy.9
  313.1 96.0 %all_to_all.19 = bf16[128,16,512]{0,2,1:T(8,128)(2,1)S(1)} all-to-all(bf16[128,16,512]{0,2,1:T(8,128)(2,1)} %bitcast.11), channel_id=1, replica_groups=mesh['row'=16,'col'=2] {'row'}, dimensions={1} | all-to-all | bytes 4194304 | tf_op jit(solution)/shard_map/all_to_all | solution.py:24
  409.0 2.6 copy.10
  411.6 0.0 copy-start.1
  411.6 38.3 %all-gather.11.cloned.1.call-done = bf16[4096,2048]{1,0:T(8,128)(2,1)} async-done(((bf16[256,2048]{1,0:T(8,128)(2,1)}), bf16[4096,2048]{1,0:T(8,128)(2,1)}) %all-gather.11.cloned.1.call-update) | async-done | bytes 16777232 | tf_op jit(solution)/shard_map/all_gather | solution.py:15
  449.9 57.4 %all-gather.9.cloned.1.call-done = bf16[512,4096]{1,0:T(8,128)(2,1)} async-done(((bf16[512,2048]{1,0:T(8,128)(2,1)}), bf16[512,4096]{1,0:T(8,128)(2,1)}) %all-gather.9.cloned.1.call-update) | async-done | bytes 4194320 | tf_op jit(solution)/shard_map/all_gather | solution.py:18
  507.3 14.2 %multiply_subtract_fusion = f32[512,2048]{1,0:T(8,128)S(1)} fusion(f32[512,2048]{1,0:T(8,128)} %param.5, bf16[512,4096]{1,0:T(8,128)(2,1)} %all-gather.9.cloned.1.call-done, bf16[4096,2048]{1,0:T(8,128)(2,1)} %all-gather.11.cloned.1.call-done), kind=kOutput, calls=%fused_computation.1 | convolution fusion | flops 8592031744 | bytes 29360128 | tf_op jit(solution)/shard_map/dot_general | solution.py:17
  521.6 0.0 copy-start.2
  521.6 2.0 copy-done.2
  523.6 0.0 copy-done.1
  523.6 8.2 %convolution_bitcast_fusion = f32[2048,2048]{0,1:T(8,128)} fusion(bf16[2048,512]{1,0:T(8,128)(2,1)S(1)} %bitcast.12, f32[512,2048]{1,0:T(8,128)S(1)} %multiply_subtract_fusion), kind=kOutput, calls=%fused_computation | convolution fusion | flops 4296015872 | bytes 23068672 | tf_op jit(solution)/shard_map/dot_general | solution.py:27
  531.7 0.0 reduce-scatter.2.cloned.1.call-update
  531.8 178.7 %reduce-scatter.2.cloned.1.call-done = f32[128,2048]{0,1:T(8,128)} async-done(((f32[2048,2048]{0,1:T(8,128)}), f32[128,2048]{0,1:T(8,128)}) %reduce-scatter.2.cloned.1.call-update) | async-done | bytes 1048592 | tf_op jit(solution)/shard_map/reduce_scatter | solution.py:26
  710.5 1.3 convert_element_type.11
  711.8 1.0 copy.11
Async XLA Ops:
  7.2 109.1 %all-gather.5.cloned.1.call-start = ((), (), s32[]{:S(2)}) async-start(), calls=%async_computation.2 | async-start | bytes 12582912 | tf_op jit(solution)/shard_map/all_gather | solution.py:8
  7.9 278.1 %all-gather.7.cloned.1.call-start = ((), (), s32[]{:S(2)}) async-start(), calls=%async_computation.3 | async-start | bytes 35651584 | tf_op jit(solution)/shard_map/all_gather | solution.py:11
  8.6 441.3 %all-gather.11.cloned.1.call-start = ((), (), s32[]{:S(2)}) async-start(), calls=%async_computation.5 | async-start | bytes 17825792 | tf_op jit(solution)/shard_map/all_gather | solution.py:15
  9.4 301.2 %copy-start = (bf16[128,8192]{1,0:T(8,128)(2,1)S(1)}, bf16[128,8192]{1,0:T(8,128)(2,1)}, u32[]{:S(2)}) copy-start(bf16[128,8192]{1,0:T(8,128)(2,1)} %param.9) | copy-start | bytes 6291460
  9.4 497.9 %all-gather.9.cloned.1.call-start = ((), (), s32[]{:S(2)}) async-start(), calls=%async_computation.4 | async-start | bytes 6291456 | tf_op jit(solution)/shard_map/all_gather | solution.py:18
  310.6 400.0 %reduce-scatter.2.cloned.1.call-start = ((), (), s32[]{:S(2)}) async-start(), calls=%async_computation.6 | async-start | bytes 17825792 | tf_op jit(solution)/shard_map/reduce_scatter | solution.py:26
  411.6 111.9 %copy-start.1 = (bf16[16,128,512]{2,1,0:T(8,128)(2,1)S(1)}, bf16[16,128,512]{2,1,0:T(8,128)(2,1)}, u32[]{:S(2)}) copy-start(bf16[16,128,512]{2,1,0:T(8,128)(2,1)} %copy.10) | copy-start | bytes 6291460
  521.6 2.0 copy-start.2
Sparse Core Ops, SparseCore 0:
  9.5 106.6 all-gather.4
  117.9 168.0 all-gather.6
  288.1 161.7 all-gather.10
  451.9 55.4 all-gather.8
  531.9 178.5 reduce-scatter.1
where the time goes:
time: 720 us; the launch traced here: 719 us
  waiting for transfers between devices  553 us (77%)
  blocking collectives  96 us (13%)
  matrix products  46.9 us (7%)
  between operations  13.8 us (2%)
  local copies, waits for them, and re-layouts  8.08 us (1%)
    reduce_scatter x1, waiting for transfers between devices, shards(): lax.psum_scatter(jnp.dot(selected, narrow, preferred_element_type=jnp.flo...  179 us
    all_gather x1, waiting for transfers between devices, shards(): lax.all_gather(grad, 'row', axis=0, tiled=True)  170 us
    all_gather x1, waiting for transfers between devices, shards(): left_panel = lax.all_gather(left, 'col', axis=1, tiled=True)  107 us
    all_to_all x1, blocking collectives, shards(): lax.all_to_all(tokens, 'row', split_axis=1, concat_axis=0, tiled=True)  96 us
    all_gather x1, waiting for transfers between devices, shards(): lax.all_gather(left_grad, 'col', axis=1, tiled=True)  57.4 us
    all_gather x1, waiting for transfers between devices, shards(): right_panel = lax.all_gather(right, 'row', axis=0, tiled=True)  38.3 us
    dot_general x1, matrix products, shards(): jnp.dot(left_panel, lax.all_gather(grad, 'row', axis=0, tiled=True), pref...  24.6 us
  transfers between devices with their start and end apart: 5, of which 5 were waited for; matrix products, arithmetic and copies ran while one was open for 4% of the time, Pallas kernels for 0%

commit v1 on v0

v1 whole, which is shorter than its diff:
```python
import jax
import jax.numpy as jnp
from jax import lax
from jax.experimental import pallas as pl
from jax.sharding import Mesh, PartitionSpec as P

F32 = jnp.float32
BF16 = jnp.bfloat16
ROWS = ("z", "y", "k")
EIGHTHS = (2, 2, 3, 1)


def shift(block, axis, size, by):
    return lax.ppermute(block, axis, [(i, (i + by) % size) for i in range(size)])


def swap(block, axis):
    return shift(block, axis, 2, 1)


def others(own, axis, size):
    return [shift(own, axis, size, -by) for by in range(1, size)]


def dot(a, b):
    return jnp.dot(a, b, preferred_element_type=F32)


def columns(array, start, width):
    return lax.dynamic_slice_in_dim(array, start, width, 1)


def tie(tree):
    arrays, form = jax.tree.flatten(tree)
    tied = pl.pallas_call(
        lambda *refs: None,
        out_shape=[jax.ShapeDtypeStruct(a.shape, a.dtype) for a in arrays],
        in_specs=[pl.BlockSpec(memory_space=pl.ANY)] * len(arrays),
        out_specs=[pl.BlockSpec(memory_space=pl.ANY)] * len(arrays),
        input_output_aliases={i: i for i in range(len(arrays))},
    )(*arrays)
    return jax.tree.unflatten(form, tied)


def lay(blocks, me, axis):
    n = len(blocks)
    if n == 2:
        a, b = blocks
        first, last = jnp.where(me == 0, a, b), jnp.where(me == 0, b, a)
        return jnp.concatenate([first, last], axis=axis)
    shape = list(blocks[0].shape)
    width, shape[axis] = shape[axis], shape[axis] * n
    whole = jnp.zeros(shape, blocks[0].dtype)
    for by, block in enumerate(blocks):
        whole = lax.dynamic_update_slice_in_dim(whole, block, (me + by) % n * width, axis)
    return whole


def chunks(width):
    parts = EIGHTHS if width % 1024 == 0 else (2, 2, 2, 2)
    ends = [sum(parts[:i]) * width // 8 for i in range(len(parts) + 1)]
    return list(zip(ends, ends[1:]))


def step(sizes, weight, grad, left, right, tokens):
    nz, nx = sizes["z"], sizes["x"]
    y, k, x, z = (lax.axis_index(a) for a in ("y", "k", "x", "z"))
    rows, width = grad.shape
    deep = right.shape[0]
    count = tokens.shape[0]
    part = count // nx
    per = nz // nx
    spans = chunks(width)

    def of_y(array, which, size):
        size *= 2
        return jnp.concatenate(
            [columns(array, (2 * i + which) * size, size) for i in range(per)], axis=1
        )

    share = lax.dynamic_slice_in_dim(tokens, x * part, part, 0)

    def piece(level):
        return jnp.concatenate(
            [
                columns(share, (level * 4 + (y ^ dy) * 2 + (k ^ dk)) * rows, rows)
                for dk in range(2)
                for dy in range(2)
            ],
            axis=1,
        )

    def gather_levels(block):
        return lax.all_gather(block, ("z", "k"), axis=0, tiled=True)

    def multiply_tokens(narrow, near):
        narrow = jnp.concatenate([narrow, near], axis=0)
        narrow = jnp.concatenate([narrow, swap(narrow, "k")], axis=0)
        sums = dot(token_panel, narrow)
        total = sums[:count]
        for by in range(1, nz):
            send = sums[by * count : (by + 1) * count].astype(BF16)
            total += shift(send, "z", nz, -by).astype(F32)
        return total.astype(BF16)

    half = width // 2
    right_panels = [gather_levels(right[:, :half])]
    grad_mine = of_y(grad, y, deep)
    spread = [piece((z + by) % nz) for by in range(nz)]
    now = tie(
        {
            "mine": grad_mine,
            "mine_x": others(grad_mine, "x", nx),
            "borrowed": swap(of_y(grad, 1 - y, deep), "y"),
            "right": right[:, half:],
            "left": [of_y(left, y, rows), of_y(left, 1 - y, rows)],
            "spread": [spread[0]]
            + [shift(spread[by], "z", nz, by) for by in range(1, nz)],
        }
    )
    right_panels.append(gather_levels(now["right"]))
    left_mine, left_lent = now["left"]
    left_mine_x = others(left_mine, "x", nx)
    left_borrowed = swap(left_lent, "y")
    grad_mine = lay([now["mine"], *now["mine_x"]], x, 1)
    grad_borrowed = lay([now["borrowed"], *others(now["borrowed"], "x", nx)], x, 1)
    spread = jnp.concatenate(now["spread"], axis=0)

    def multiply(start, stop):
        which = start // half
        panel = right_panels[which][:, start - which * half : stop - which * half]
        received = swap(dot(grad_borrowed, panel).astype(BF16), "y")
        own = dot(grad_mine, panel) + received.astype(F32)
        return own.astype(BF16)

    product = multiply(*spans[0])
    now = tie(
        {
            "product": product,
            "grad": grad_borrowed,
            "mine_x": left_mine_x,
            "mine": left_mine,
            "borrowed": left_borrowed,
            "spread": spread,
        }
    )
    grad_borrowed = now["grad"]
    products = [now["product"]] + [multiply(*span) for span in spans[1:]]
    left_mine = lay([now["mine"], *now["mine_x"]], x, 1)
    left_borrowed = lay([now["borrowed"], *others(now["borrowed"], "x", nx)], x, 1)
    spread = now["spread"]
    token_panel = lay(
        [b.reshape(nz, part, 4 * rows) for b in [spread, *others(spread, "x", nx)]], x, 1
    ).reshape(nz * count, 4 * rows)

    new_weight, outputs = weight, []
    near = None
    for (start, stop), product in zip(spans, products):
        panel = gather_levels(product)
        if near is not None:
            panel, near = tie((panel, near))
            outputs.append(multiply_tokens(narrow, near))
        received = swap(dot(left_borrowed, panel).astype(BF16), "y")
        precond = dot(left_mine, panel) + received.astype(F32)
        update = weight[:, start:stop] - 0.01 * precond
        new_weight = lax.dynamic_update_slice(new_weight, update, (0, start))
        narrow = update.astype(BF16)
        near = swap(narrow, "y")
    outputs.append(multiply_tokens(narrow, near))
    return new_weight, jnp.concatenate(outputs, axis=1)


def solution(mesh):
    nrow, ncol = mesh.shape["row"], mesh.shape["col"]
    sizes = {"z": nrow // 4, "y": 2, "k": 2, "x": ncol}
    fine = Mesh(mesh.devices.reshape(nrow // 4, 2, 2, ncol), ("z", "y", "k", "x"))
    split = P(ROWS, "x")
    return jax.shard_map(
        lambda *args: step(sizes, *args),
        mesh=fine,
        in_specs=(split, split, split, split, P(ROWS, None)),
        out_specs=(split, split),
        check_vma=False,
    )
```

time: 720 us -> 430 us (0.60)
  waiting for transfers between devices: 553 us -> 248 us
  blocking collectives: 96 us -> 0 us
  starting transfers between devices: 0.19 us -> 45 us
  other arithmetic: 1.28 us -> 29.4 us
  matrix products: 46.9 us -> 74.1 us
  local copies, waits for them, and re-layouts: 8.08 us -> 18.9 us
    all_gather x4 -> x6, waiting for transfers between devices: 372 us -> 28.9 us  [gather_levels(): return lax.all_gather(block, ('z', 'k'), axis=0, tiled=True)]
    ppermute x0 -> x38, waiting for transfers between devices: none -> 219 us  [shift(): lax.ppermute(block, axis, [(i, (i + by) % size) for i in range(size)])]
    reduce_scatter x1 -> x0, waiting for transfers between devices: 179 us -> none  [shards(): lax.psum_scatter(jnp.dot(selected, narrow, preferred_element_type=jnp.flo...]
    all_to_all x1 -> x0, blocking collectives: 96 us -> none  [shards(): lax.all_to_all(tokens, 'row', split_axis=1, concat_axis=0, tiled=True)]
    ppermute x0 -> x38, starting transfers between devices: none -> 44.6 us  [shift(): lax.ppermute(block, axis, [(i, (i + by) % size) for i in range(size)])]
    dot_general x3 -> x20, matrix products: 46.9 us -> 74.1 us  [dot(): return jnp.dot(a, b, preferred_element_type=F32)]
    concatenate x0 -> x15, other arithmetic: none -> 15.7 us  [the longest x4 4.61 us: multiply_tokens(): narrow = jnp.concatenate([narrow, near], axis=0)]
    select_n x0 -> x5, other arithmetic: none -> 10.3 us  [lay(): first, last = (jnp.where(me == 0, a, b), jnp.where(me == 0, b, a))]
  transfers between devices with their start and end apart: 5 -> 44, of which waited for: 5 -> 23; matrix products, arithmetic and copies ran while one was open for 4% -> 27% of each run, Pallas kernels for 0% -> 0%
where the time goes in v1:
time: 430 us
  waiting for transfers between devices  248 us (58%)
  matrix products  74.1 us (17%)
  starting transfers between devices  45 us (10%)
  other arithmetic  29.4 us (7%)
  local copies, waits for them, and re-layouts  18.9 us (4%)
  between operations  14.9 us (3%)
    ppermute x38, waiting for transfers between devices, shift(): lax.ppermute(block, axis, [(i, (i + by) % size) for i in range(size)])  219 us
    dot_general x20, matrix products, dot(): return jnp.dot(a, b, preferred_element_type=F32)  74.1 us
    ppermute x38, starting transfers between devices, shift(): lax.ppermute(block, axis, [(i, (i + by) % size) for i in range(size)])  44.6 us
    all_gather x6, waiting for transfers between devices, gather_levels(): return lax.all_gather(block, ('z', 'k'), axis=0, tiled=True)  28.9 us
    select_n x5, other arithmetic, lay(): first, last = (jnp.where(me == 0, a, b), jnp.where(me == 0, b, a))  10.3 us
  transfers between devices with their start and end apart: 44, of which 23 were waited for; matrix products, arithmetic and copies ran while one was open for 27% of the time, Pallas kernels for 0%

profile of v1, /device:TPU:0, one launch (start us, length us, event | category | flops | bytes accessed | tf_op | source)
XLA Modules:
  0.0 429.9 jit_solution(6519664780880189542)
XLA Ops:
  32.5 16.8 %collective-permute-done.3.refs_8_ = bf16[64,2048]{1,0:T(8,128)(2,1)} collective-permute-done((bf16[64,2048]{1,0:T(8,128)(2,1)}, bf16[64,2048]{1,0:T(8,128)(2,1)}, u32[]{:S(2)}, u32[]{:S(2)}) %collective-permute-start.3) | collective-permute-done | bytes 262176 | tf_op jit(solution)/shard_map/ppermute | solution.py:14
  58.5 20.5 %collective-permute-done.6 = bf16[512,1024]{1,0:T(8,128)(2,1)} collective-permute-done((bf16[512,1024]{1,0:T(8,128)(2,1)}, bf16[512,1024]{1,0:T(8,128)(2,1)}, u32[]{:S(2)}, u32[]{:S(2)}) %collective-permute-start.6) | collective-permute-done | bytes 1048608 | tf_op jit(solution)/shard_map/ppermute | solution.py:14
  81.4 3.3 fusion.45
  89.3 20.5 %collective-permute-done.8 = bf16[512,512]{1,0:T(8,128)(2,1)S(1)} collective-permute-done((bf16[512,512]{1,0:T(8,128)(2,1)S(1)}, bf16[512,512]{1,0:T(8,128)(2,1)S(1)}, u32[]{:S(2)}, u32[]{:S(2)}) %collective-permute-start.8) | collective-permute-done | bytes 524320 | tf_op jit(solution)/shard_map/ppermute | solution.py:14
  111.9 9.2 %collective-permute-done.7.refs_3_ = bf16[512,2048]{1,0:T(8,128)(2,1)} collective-permute-done((bf16[512,2048]{1,0:T(8,128)(2,1)}, bf16[512,2048]{1,0:T(8,128)(2,1)}, u32[]{:S(2)}, u32[]{:S(2)}) %collective-permute-start.7) | collective-permute-done | bytes 2097184 | tf_op jit(solution)/shard_map/ppermute | solution.py:14
  121.2 3.7 fusion.48
  125.0 11.1 %collective-permute-done.11 = bf16[512,512]{1,0:T(8,128)(2,1)S(1)} collective-permute-done((bf16[512,512]{1,0:T(8,128)(2,1)S(1)}, bf16[512,512]{1,0:T(8,128)(2,1)S(1)}, u32[]{:S(2)}, u32[]{:S(2)}) %collective-permute-start.11) | collective-permute-done | bytes 524320 | tf_op jit(solution)/shard_map/ppermute | solution.py:14
  138.3 3.8 fusion.32
  142.5 15.5 %collective-permute-done.14 = bf16[512,768]{1,0:T(8,128)(2,1)S(1)} collective-permute-done((bf16[512,768]{1,0:T(8,128)(2,1)S(1)}, bf16[512,768]{1,0:T(8,128)(2,1)S(1)}, u32[]{:S(2)}, u32[]{:S(2)}) %collective-permute-start.14) | collective-permute-done | bytes 786464 | tf_op jit(solution)/shard_map/ppermute | solution.py:14
  162.2 4.8 %copy.50 = f32[512,2048]{1,0:T(8,128)} copy(f32[512,2048]{1,0:T(8,128)} %param.5) | data formatting | bytes 8388608
  166.9 37.5 %collective-permute-done.9 = bf16[512,2048]{1,0:T(8,128)(2,1)S(1)} collective-permute-done((bf16[512,2048]{1,0:T(8,128)(2,1)}, bf16[512,2048]{1,0:T(8,128)(2,1)S(1)}, u32[]{:S(2)}, u32[]{:S(2)}) %collective-permute-start.9) | collective-permute-done | bytes 2097184 | tf_op jit(solution)/shard_map/ppermute | solution.py:14
  206.7 6.0 %convolution_convert_fusion.2 = bf16[512,512]{1,0:T(8,128)(2,1)S(1)} fusion(bf16[4096,512]{1,0:T(8,128)(2,1)} %all-gather.9.cloned.1.call-done, bf16[512,2048]{1,0:T(8,128)(2,1)} %get-tuple-element.49, bf16[512,2048]{1,0:T(8,128)(2,1)} %get-tuple-element.48), kind=kOutput, calls=%fused_computation.57 | convolution fusion | flops 2156134400 | bytes 8912896 | tf_op jit(solution)/shard_map/dot_general | solution.py:26
  216.7 5.3 %collective-permute-done.10 = bf16[512,512]{1,0:T(8,128)(2,1)S(1)} collective-permute-done((bf16[512,512]{1,0:T(8,128)(2,1)S(1)}, bf16[512,512]{1,0:T(8,128)(2,1)S(1)}, u32[]{:S(2)}, u32[]{:S(2)}) %collective-permute-start.10) | collective-permute-done | bytes 524320 | tf_op jit(solution)/shard_map/ppermute | solution.py:14
  222.0 3.6 fusion.43
  230.8 5.2 %collective-permute-done.12.refs_1_ = bf16[512,512]{1,0:T(8,128)(2,1)S(1)} collective-permute-done((bf16[512,512]{1,0:T(8,128)(2,1)S(1)}, bf16[512,512]{1,0:T(8,128)(2,1)S(1)}, u32[]{:S(2)}, u32[]{:S(2)}) %collective-permute-start.12) | collective-permute-done | bytes 524320 | tf_op jit(solution)/shard_map/ppermute | solution.py:14
  236.7 6.9 %convolution_convert_fusion.1 = bf16[512,512]{1,0:T(8,128)(2,1)S(1)} fusion(bf16[4096,512]{1,0:T(8,128)(2,1)} %get-tuple-element.38, bf16[512,2048]{1,0:T(8,128)(2,1)} %get-tuple-element.49, bf16[512,2048]{1,0:T(8,128)(2,1)} %get-tuple-element.48), kind=kOutput, calls=%fused_computation.56 | convolution fusion | flops 2156134400 | bytes 8912896 | tf_op jit(solution)/shard_map/dot_general | solution.py:26
  246.5 8.4 %collective-permute-done.13 = bf16[512,512]{1,0:T(8,128)(2,1)S(1)} collective-permute-done((bf16[512,512]{1,0:T(8,128)(2,1)S(1)}, bf16[512,512]{1,0:T(8,128)(2,1)S(1)}, u32[]{:S(2)}, u32[]{:S(2)}) %collective-permute-start.13) | collective-permute-done | bytes 524320 | tf_op jit(solution)/shard_map/ppermute | solution.py:14
  254.9 4.9 %fusion.86 = (bf16[512,512]{1,0:T(8,128)(2,1)}, f32[512,2048]{1,0:T(8,128)}) fusion(f32[512,2048]{1,0:T(8,128)} %get-tuple-element.85, bf16[512,512]{1,0:T(8,128)(2,1)S(1)} %collective-permute-done.13, bf16[4096,512]{1,0:T(8,128)(2,1)S(1)} %copy-done.10, bf16[512,2048]{1,0:T(8,128)(2,1)S(1)} %copy-done.24, bf16[512,2048]{1,0:T(8,128)(2,1)S(1)} %copy-done.20, ...), kind=kOutput, calls=%fused_computation.126 | convolution fusion | flops 2157182976 | bytes 11534336 | tf_op jit(solution)/shard_map/dot_general | solution.py:26
  264.3 4.9 %collective-permute-done.15.refs_1_ = bf16[512,512]{1,0:T(8,128)(2,1)S(1)} collective-permute-done((bf16[512,512]{1,0:T(8,128)(2,1)}, bf16[512,512]{1,0:T(8,128)(2,1)S(1)}, u32[]{:S(2)}, u32[]{:S(2)}) %collective-permute-start.15) | collective-permute-done | bytes 524320 | tf_op jit(solution)/shard_map/ppermute | solution.py:14
  269.2 26.6 %all-gather.15.cloned.1.call-done.refs_0_ = bf16[4096,768]{1,0:T(8,128)(2,1)} async-done(((bf16[512,768]{1,0:T(8,128)(2,1)}), bf16[4096,768]{1,0:T(8,128)(2,1)}) %all-gather.15.cloned.1.call-update) | async-done | bytes 6291472 | tf_op jit(solution)/shard_map/all_gather | solution.py:94
  295.8 7.6 %convolution_convert_fusion = bf16[512,768]{1,0:T(8,128)(2,1)S(1)} fusion(bf16[4096,768]{1,0:T(8,128)(2,1)} %get-tuple-element.40, bf16[512,2048]{1,0:T(8,128)(2,1)} %get-tuple-element.49, bf16[512,2048]{1,0:T(8,128)(2,1)} %get-tuple-element.48), kind=kOutput, calls=%fused_computation.45 | convolution fusion | flops 3230007296 | bytes 11272192 | tf_op jit(solution)/shard_map/dot_general | solution.py:26
  305.2 17.9 %collective-permute-done.16 = bf16[512,768]{1,0:T(8,128)(2,1)S(1)} collective-permute-done((bf16[512,768]{1,0:T(8,128)(2,1)S(1)}, bf16[512,768]{1,0:T(8,128)(2,1)S(1)}, u32[]{:S(2)}, u32[]{:S(2)}) %collective-permute-start.16) | collective-permute-done | bytes 786464 | tf_op jit(solution)/shard_map/ppermute | solution.py:14
  323.2 6.6 %fusion.85 = (bf16[512,768]{1,0:T(8,128)(2,1)}, f32[512,2048]{1,0:T(8,128)}) fusion(f32[512,2048]{1,0:T(8,128)} %get-tuple-element.83, bf16[512,768]{1,0:T(8,128)(2,1)S(1)} %collective-permute-done.16, bf16[4096,768]{1,0:T(8,128)(2,1)S(1)} %copy-done.6, bf16[512,2048]{1,0:T(8,128)(2,1)S(1)} %copy-done.25, bf16[512,2048]{1,0:T(8,128)(2,1)S(1)} %copy-done.21, ...), kind=kOutput, calls=%fused_computation.125 | convolution fusion | flops 3231580160 | bytes 15204352 | tf_op jit(solution)/shard_map/dot_general | solution.py:26
  335.9 13.0 %collective-permute-done.18.refs_1_ = bf16[512,768]{1,0:T(8,128)(2,1)S(1)} collective-permute-done((bf16[512,768]{1,0:T(8,128)(2,1)}, bf16[512,768]{1,0:T(8,128)(2,1)S(1)}, u32[]{:S(2)}, u32[]{:S(2)}) %collective-permute-start.18) | collective-permute-done | bytes 786464 | tf_op jit(solution)/shard_map/ppermute | solution.py:14
  349.8 4.3 convolution_convert_fusion.3
  365.6 3.7 fusion.96
  369.3 3.9 collective-permute-done.33
  380.8 4.1 collective-permute-done.28
  384.9 5.5 %collective-permute-done.27 = bf16[128,512]{0,1:T(8,128)(2,1)} collective-permute-done((bf16[128,512]{0,1:T(8,128)(2,1)}, bf16[128,512]{0,1:T(8,128)(2,1)}, u32[]{:S(2)}, u32[]{:S(2)}) %collective-permute-start.27) | collective-permute-done | bytes 131104 | tf_op jit(solution)/shard_map/ppermute | solution.py:14
  396.8 3.4 fusion.95
  405.6 6.4 %collective-permute-done.30 = bf16[128,768]{1,0:T(8,128)(2,1)S(1)} collective-permute-done((bf16[128,768]{1,0:T(8,128)(2,1)S(1)}, bf16[128,768]{1,0:T(8,128)(2,1)S(1)}, u32[]{:S(2)}, u32[]{:S(2)}) %collective-permute-start.30) | collective-permute-done | bytes 196640 | tf_op jit(solution)/shard_map/ppermute | solution.py:14
  413.8 8.3 %collective-permute-done.31 = bf16[128,768]{1,0:T(8,128)(2,1)S(1)} collective-permute-done((bf16[128,768]{1,0:T(8,128)(2,1)S(1)}, bf16[128,768]{1,0:T(8,128)(2,1)S(1)}, u32[]{:S(2)}, u32[]{:S(2)}) %collective-permute-start.31) | collective-permute-done | bytes 196640 | tf_op jit(solution)/shard_map/ppermute | solution.py:14
  (241 shorter events, 112.2 us)
Async XLA Ops:
  7.2 74.3 %all-gather.7.cloned.1.call-start = ((), (), s32[]{:S(2)}) async-start(), calls=%async_computation | async-start | bytes 4718592 | tf_op jit(solution)/shard_map/all_gather | solution.py:94
  9.5 128.8 %all-gather.13.cloned.1.call-start = ((), (), s32[]{:S(2)}) async-start(), calls=%async_computation.3 | async-start | bytes 4718592 | tf_op jit(solution)/shard_map/all_gather | solution.py:94
  13.7 18.8 %collective-permute-start.2 = (bf16[64,2048]{1,0:T(8,128)(2,1)}, bf16[64,2048]{1,0:T(8,128)(2,1)S(1)}, u32[]{:S(2)}, u32[]{:S(2)}) collective-permute-start(bf16[64,2048]{1,0:T(8,128)(2,1)} %pad_maximum_fusion.16), channel_id=1, source_target_pairs={{0,8},{8,16},{16,24},{24,0},{1,9},{9,17},{17,25},{25,1},{2,10},{10... | collective-permute-start | bytes 786440 | tf_op jit(solution)/shard_map/ppermute | solution.py:14
  18.1 32.9 %collective-permute-start = (bf16[512,1024]{1,0:T(8,128)(2,1)}, bf16[512,1024]{1,0:T(8,128)(2,1)S(1)}, u32[]{:S(2)}, u32[]{:S(2)}) collective-permute-start(bf16[512,1024]{1,0:T(8,128)(2,1)} %pad_maximum_fusion.8), channel_id=1, source_target_pairs={{0,4},{4,0},{1,5},{5,1},{2,6},{6,2},{3,7},{7,3},{8,12},{12,8},{9,1... | collective-permute-start | bytes 3145736 | tf_op jit(solution)/shard_map/ppermute | solution.py:14
  19.8 31.2 %collective-permute-start.1 = (bf16[512,1024]{1,0:T(8,128)(2,1)S(1)}, bf16[512,1024]{1,0:T(8,128)(2,1)S(1)}, u32[]{:S(2)}, u32[]{:S(2)}) collective-permute-start(bf16[512,1024]{1,0:T(8,128)(2,1)S(1)} %pad_maximum_fusion.9.refs_3_), channel_id=1, source_target_pairs={{0,1},{1,0},{2,3},{3,2},{4,5},{5,4},{6,7},{7,6},{8,9},{9,8},{10,11... | collective-permute-start | bytes 3145736 | tf_op jit(solution)/shard_map/ppermute | solution.py:14
  22.0 27.2 %collective-permute-start.3 = (bf16[64,2048]{1,0:T(8,128)(2,1)}, bf16[64,2048]{1,0:T(8,128)(2,1)}, u32[]{:S(2)}, u32[]{:S(2)}) collective-permute-start(bf16[64,2048]{1,0:T(8,128)(2,1)} %pad_maximum_fusion.17), channel_id=1, source_target_pairs={{0,16},{8,24},{16,0},{24,8},{1,17},{9,25},{17,1},{25,9},{2,18},{10... | collective-permute-start | bytes 786440 | tf_op jit(solution)/shard_map/ppermute | solution.py:14
  25.4 25.6 %collective-permute-start.4 = (bf16[64,2048]{1,0:T(8,128)(2,1)}, bf16[64,2048]{1,0:T(8,128)(2,1)}, u32[]{:S(2)}, u32[]{:S(2)}) collective-permute-start(bf16[64,2048]{1,0:T(8,128)(2,1)} %pad_maximum_fusion.18), channel_id=1, source_target_pairs={{0,24},{8,0},{16,8},{24,16},{1,25},{9,1},{17,9},{25,17},{2,26},{10... | collective-permute-start | bytes 786440 | tf_op jit(solution)/shard_map/ppermute | solution.py:14
  52.5 154.2 %all-gather.9.cloned.1.call-start = ((), (), s32[]{:S(2)}) async-start(), calls=%async_computation.1 | async-start | bytes 4718592 | tf_op jit(solution)/shard_map/all_gather | solution.py:94
  52.5 26.5 %collective-permute-start.6 = (bf16[512,1024]{1,0:T(8,128)(2,1)}, bf16[512,1024]{1,0:T(8,128)(2,1)}, u32[]{:S(2)}, u32[]{:S(2)}) collective-permute-start(bf16[512,1024]{1,0:T(8,128)(2,1)} %get-tuple-element.25), channel_id=1, source_target_pairs={{0,1},{1,0},{2,3},{3,2},{4,5},{5,4},{6,7},{7,6},{8,9},{9,8},{10,11... | collective-permute-start | bytes 3145736 | tf_op jit(solution)/shard_map/ppermute | solution.py:14
  53.4 58.5 %collective-permute-start.5 = (bf16[512,2048]{1,0:T(8,128)(2,1)}, bf16[512,2048]{1,0:T(8,128)(2,1)S(1)}, u32[]{:S(2)}, u32[]{:S(2)}) collective-permute-start(bf16[512,2048]{1,0:T(8,128)(2,1)} %get-tuple-element.24), channel_id=1, source_target_pairs={{0,4},{4,0},{1,5},{5,1},{2,6},{6,2},{3,7},{7,3},{8,12},{12,8},{9,1... | collective-permute-start | bytes 6291464 | tf_op jit(solution)/shard_map/ppermute | solution.py:14
  53.8 67.3 %collective-permute-start.7 = (bf16[512,2048]{1,0:T(8,128)(2,1)}, bf16[512,2048]{1,0:T(8,128)(2,1)}, u32[]{:S(2)}, u32[]{:S(2)}) collective-permute-start(bf16[512,2048]{1,0:T(8,128)(2,1)} %get-tuple-element.26.refs_2_), channel_id=1, source_target_pairs={{0,1},{1,0},{2,3},{3,2},{4,5},{5,4},{6,7},{7,6},{8,9},{9,8},{10,11... | collective-permute-start | bytes 6291464 | tf_op jit(solution)/shard_map/ppermute | solution.py:14
  84.8 25.1 %collective-permute-start.8 = (bf16[512,512]{1,0:T(8,128)(2,1)S(1)}, bf16[512,512]{1,0:T(8,128)(2,1)S(1)}, u32[]{:S(2)}, u32[]{:S(2)}) collective-permute-start(bf16[512,512]{1,0:T(8,128)(2,1)S(1)} %fusion.45), channel_id=1, source_target_pairs={{0,4},{4,0},{1,5},{5,1},{2,6},{6,2},{3,7},{7,3},{8,12},{12,8},{9,1... | collective-permute-start | bytes 1572872 | tf_op jit(solution)/shard_map/ppermute | solution.py:14
  121.2 109.6 %all-gather.11.cloned.1.call-start = ((), (), s32[]{:S(2)}) async-start(), calls=%async_computation.2 | async-start | bytes 4718592 | tf_op jit(solution)/shard_map/all_gather | solution.py:94
  138.2 157.6 %all-gather.15.cloned.1.call-start = ((), (), s32[]{:S(2)}) async-start(), calls=%async_computation.4 | async-start | bytes 7077888 | tf_op jit(solution)/shard_map/all_gather | solution.py:94
  142.1 15.9 %collective-permute-start.14 = (bf16[512,768]{1,0:T(8,128)(2,1)S(1)}, bf16[512,768]{1,0:T(8,128)(2,1)S(1)}, u32[]{:S(2)}, u32[]{:S(2)}) collective-permute-start(bf16[512,768]{1,0:T(8,128)(2,1)S(1)} %fusion.32), channel_id=1, source_target_pairs={{0,4},{4,0},{1,5},{5,1},{2,6},{6,2},{3,7},{7,3},{8,12},{12,8},{9,1... | collective-permute-start | bytes 2359304 | tf_op jit(solution)/shard_map/ppermute | solution.py:14
  160.8 175.1 %all-gather.17.cloned.1.call-start = ((), (), s32[]{:S(2)}) async-start(), calls=%async_computation.5 | async-start | bytes 2359296 | tf_op jit(solution)/shard_map/all_gather | solution.py:94
  161.1 43.3 %collective-permute-start.9 = (bf16[512,2048]{1,0:T(8,128)(2,1)}, bf16[512,2048]{1,0:T(8,128)(2,1)S(1)}, u32[]{:S(2)}, u32[]{:S(2)}) collective-permute-start(bf16[512,2048]{1,0:T(8,128)(2,1)} %get-tuple-element.36), channel_id=1, source_target_pairs={{0,1},{1,0},{2,3},{3,2},{4,5},{5,4},{6,7},{7,6},{8,9},{9,8},{10,11... | collective-permute-start | bytes 6291464 | tf_op jit(solution)/shard_map/ppermute | solution.py:14
  243.6 11.3 %collective-permute-start.13 = (bf16[512,512]{1,0:T(8,128)(2,1)S(1)}, bf16[512,512]{1,0:T(8,128)(2,1)S(1)}, u32[]{:S(2)}, u32[]{:S(2)}) collective-permute-start(bf16[512,512]{1,0:T(8,128)(2,1)S(1)} %convolution_convert_fusion.1), channel_id=1, source_target_pairs={{0,4},{4,0},{1,5},{5,1},{2,6},{6,2},{3,7},{7,3},{8,12},{12,8},{9,1... | collective-permute-start | bytes 1572872 | tf_op jit(solution)/shard_map/ppermute | solution.py:14
  246.1 15.1 %collective-permute-start.17 = (bf16[512,256]{1,0:T(8,128)(2,1)S(1)}, bf16[512,256]{1,0:T(8,128)(2,1)S(1)}, u32[]{:S(2)}, u32[]{:S(2)}) collective-permute-start(bf16[512,256]{1,0:T(8,128)(2,1)S(1)} %convolution_convert_fusion.4), channel_id=1, source_target_pairs={{0,4},{4,0},{1,5},{5,1},{2,6},{6,2},{3,7},{7,3},{8,12},{12,8},{9,1... | collective-permute-start | bytes 786440 | tf_op jit(solution)/shard_map/ppermute | solution.py:14
  262.7 42.2 %collective-permute-start.20 = (bf16[256,2048]{1,0:T(8,128)(2,1)S(1)}, bf16[256,2048]{1,0:T(8,128)(2,1)S(1)}, u32[]{:S(2)}, u32[]{:S(2)}) collective-permute-start(bf16[256,2048]{1,0:T(8,128)(2,1)S(1)} %copy-done.2), channel_id=1, source_target_pairs={{0,1},{1,0},{2,3},{3,2},{4,5},{5,4},{6,7},{7,6},{8,9},{9,8},{10,11... | collective-permute-start | bytes 3145736 | tf_op jit(solution)/shard_map/ppermute | solution.py:14
  303.4 19.8 %collective-permute-start.16 = (bf16[512,768]{1,0:T(8,128)(2,1)S(1)}, bf16[512,768]{1,0:T(8,128)(2,1)S(1)}, u32[]{:S(2)}, u32[]{:S(2)}) collective-permute-start(bf16[512,768]{1,0:T(8,128)(2,1)S(1)} %convolution_convert_fusion), channel_id=1, source_target_pairs={{0,4},{4,0},{1,5},{5,1},{2,6},{6,2},{3,7},{7,3},{8,12},{12,8},{9,1... | collective-permute-start | bytes 2359304 | tf_op jit(solution)/shard_map/ppermute | solution.py:14
  305.2 26.2 %collective-permute-start.21 = (bf16[1024,512]{1,0:T(8,128)(2,1)S(1)}, bf16[1024,512]{1,0:T(8,128)(2,1)S(1)}, u32[]{:S(2)}, u32[]{:S(2)}) collective-permute-start(bf16[1024,512]{1,0:T(8,128)(2,1)S(1)} %pad_maximum_fusion.11), channel_id=1, source_target_pairs={{0,2},{2,0},{1,3},{3,1},{4,6},{6,4},{5,7},{7,5},{8,10},{10,8},{9,1... | collective-permute-start | bytes 3145736 | tf_op jit(solution)/shard_map/ppermute | solution.py:14
  329.7 19.2 %collective-permute-start.18 = (bf16[512,768]{1,0:T(8,128)(2,1)}, bf16[512,768]{1,0:T(8,128)(2,1)S(1)}, u32[]{:S(2)}, u32[]{:S(2)}) collective-permute-start(bf16[512,768]{1,0:T(8,128)(2,1)} %get-tuple-element.80), channel_id=1, source_target_pairs={{0,4},{4,0},{1,5},{5,1},{2,6},{6,2},{3,7},{7,3},{8,12},{12,8},{9,1... | collective-permute-start | bytes 2359304 | tf_op jit(solution)/shard_map/ppermute | solution.py:14
  335.9 28.5 %collective-permute-start.25 = (bf16[1024,512]{1,0:T(8,128)(2,1)}, bf16[1024,512]{1,0:T(8,128)(2,1)}, u32[]{:S(2)}, u32[]{:S(2)}) collective-permute-start(bf16[1024,512]{1,0:T(8,128)(2,1)} %pad_maximum_fusion.12), channel_id=1, source_target_pairs={{0,2},{2,0},{1,3},{3,1},{4,6},{6,4},{5,7},{7,5},{8,10},{10,8},{9,1... | collective-permute-start | bytes 3145736 | tf_op jit(solution)/shard_map/ppermute | solution.py:14
  355.7 18.4 %collective-permute-start.22 = (bf16[128,512]{0,1:T(8,128)(2,1)S(1)}, bf16[128,512]{0,1:T(8,128)(2,1)S(1)}, u32[]{:S(2)}, u32[]{:S(2)}) collective-permute-start(bf16[128,512]{0,1:T(8,128)(2,1)S(1)} %get-tuple-element.91), channel_id=1, source_target_pairs={{0,24},{8,0},{16,8},{24,16},{1,25},{9,1},{17,9},{25,17},{2,26},{10... | collective-permute-start | bytes 393224 | tf_op jit(solution)/shard_map/ppermute | solution.py:14
  356.7 19.1 %collective-permute-start.24 = (bf16[128,512]{0,1:T(8,128)(2,1)S(1)}, bf16[128,512]{0,1:T(8,128)(2,1)S(1)}, u32[]{:S(2)}, u32[]{:S(2)}) collective-permute-start(bf16[128,512]{0,1:T(8,128)(2,1)S(1)} %get-tuple-element.92), channel_id=1, source_target_pairs={{0,8},{8,16},{16,24},{24,0},{1,9},{9,17},{17,25},{25,1},{2,10},{10... | collective-permute-start | bytes 393224 | tf_op jit(solution)/shard_map/ppermute | solution.py:14
  357.8 18.6 %collective-permute-start.23 = (bf16[128,512]{0,1:T(8,128)(2,1)S(1)}, bf16[128,512]{0,1:T(8,128)(2,1)S(1)}, u32[]{:S(2)}, u32[]{:S(2)}) collective-permute-start(bf16[128,512]{0,1:T(8,128)(2,1)S(1)} %get-tuple-element.93), channel_id=1, source_target_pairs={{0,16},{8,24},{16,0},{24,8},{1,17},{9,25},{17,1},{25,9},{2,18},{10... | collective-permute-start | bytes 393224 | tf_op jit(solution)/shard_map/ppermute | solution.py:14
  361.2 35.5 %collective-permute-start.29 = (bf16[1024,768]{1,0:T(8,128)(2,1)}, bf16[1024,768]{1,0:T(8,128)(2,1)}, u32[]{:S(2)}, u32[]{:S(2)}) collective-permute-start(bf16[1024,768]{1,0:T(8,128)(2,1)} %pad_maximum_fusion.7), channel_id=1, source_target_pairs={{0,2},{2,0},{1,3},{3,1},{4,6},{6,4},{5,7},{7,5},{8,10},{10,8},{9,1... | collective-permute-start | bytes 4718600 | tf_op jit(solution)/shard_map/ppermute | solution.py:14
  373.2 19.2 %collective-permute-start.34 = (bf16[1024,256]{1,0:T(8,128)(2,1)S(1)}, bf16[1024,256]{1,0:T(8,128)(2,1)}, u32[]{:S(2)}, u32[]{:S(2)}) collective-permute-start(bf16[1024,256]{1,0:T(8,128)(2,1)S(1)} %pad_maximum_fusion.13), channel_id=1, source_target_pairs={{0,2},{2,0},{1,3},{3,1},{4,6},{6,4},{5,7},{7,5},{8,10},{10,8},{9,1... | collective-permute-start | bytes 1572872 | tf_op jit(solution)/shard_map/ppermute | solution.py:14
  376.4 14.0 %collective-permute-start.27 = (bf16[128,512]{0,1:T(8,128)(2,1)}, bf16[128,512]{0,1:T(8,128)(2,1)}, u32[]{:S(2)}, u32[]{:S(2)}) collective-permute-start(bf16[128,512]{0,1:T(8,128)(2,1)} %get-tuple-element.96), channel_id=1, source_target_pairs={{0,16},{8,24},{16,0},{24,8},{1,17},{9,25},{17,1},{25,9},{2,18},{10... | collective-permute-start | bytes 393224 | tf_op jit(solution)/shard_map/ppermute | solution.py:14
  400.2 11.8 %collective-permute-start.30 = (bf16[128,768]{1,0:T(8,128)(2,1)S(1)}, bf16[128,768]{1,0:T(8,128)(2,1)S(1)}, u32[]{:S(2)}, u32[]{:S(2)}) collective-permute-start(bf16[128,768]{1,0:T(8,128)(2,1)S(1)} %get-tuple-element.88), channel_id=1, source_target_pairs={{0,24},{8,0},{16,8},{24,16},{1,25},{9,1},{17,9},{25,17},{2,26},{10... | collective-permute-start | bytes 589832 | tf_op jit(solution)/shard_map/ppermute | solution.py:14
  404.1 18.0 %collective-permute-start.31 = (bf16[128,768]{1,0:T(8,128)(2,1)S(1)}, bf16[128,768]{1,0:T(8,128)(2,1)S(1)}, u32[]{:S(2)}, u32[]{:S(2)}) collective-permute-start(bf16[128,768]{1,0:T(8,128)(2,1)S(1)} %get-tuple-element.90), channel_id=1, source_target_pairs={{0,16},{8,24},{16,0},{24,8},{1,17},{9,25},{17,1},{25,9},{2,18},{10... | collective-permute-start | bytes 589832 | tf_op jit(solution)/shard_map/ppermute | solution.py:14
  (71 other events, 782.7 us)
Sparse Core Ops, SparseCore 0:
  10.2 67.1 all-gather.6
  79.0 46.5 all-gather.12
  127.7 55.6 all-gather.8
  184.9 45.8 all-gather.10
  232.3 63.4 all-gather.14
  297.2 27.7 all-gather.16

commit v2 on v1

v2 whole, which is shorter than its diff:
```python
import jax
import jax.numpy as jnp
from jax import lax
from jax.experimental import pallas as pl
from jax.sharding import Mesh, PartitionSpec as P

F32 = jnp.float32
BF16 = jnp.bfloat16
ROWS = ("z", "y", "k")
SIXTEENTHS = (4, 4, 5, 3)


def shift(block, axis, size, by):
    return lax.ppermute(block, axis, [(i, (i + by) % size) for i in range(size)])


def swap(block, axis):
    return shift(block, axis, 2, 1)


def others(own, axis, size):
    return [shift(own, axis, size, -by) for by in range(1, size)]


def dot(a, b):
    return jnp.dot(a, b, preferred_element_type=F32)


def columns(array, start, width):
    return lax.dynamic_slice_in_dim(array, start, width, 1)


def tie(tree):
    arrays, form = jax.tree.flatten(tree)
    tied = pl.pallas_call(
        lambda *refs: None,
        out_shape=[jax.ShapeDtypeStruct(a.shape, a.dtype) for a in arrays],
        in_specs=[pl.BlockSpec(memory_space=pl.ANY)] * len(arrays),
        out_specs=[pl.BlockSpec(memory_space=pl.ANY)] * len(arrays),
        input_output_aliases={i: i for i in range(len(arrays))},
    )(*arrays)
    return jax.tree.unflatten(form, tied)


def place(whole, blocks, me, row):
    width = blocks[0].shape[1]
    for by, block in enumerate(blocks):
        column = (me + by) % len(blocks) * width
        whole = lax.dynamic_update_slice(whole, block, (row, column))
    return whole


def chunks(width):
    parts = SIXTEENTHS if width % 2048 == 0 else (8, 8)
    ends = [sum(parts[:i]) * width // 16 for i in range(len(parts) + 1)]
    return list(zip(ends, ends[1:]))


def step(sizes, weight, grad, left, right, tokens):
    nz, nx = sizes["z"], sizes["x"]
    y, k, x, z = (lax.axis_index(a) for a in ("y", "k", "x", "z"))
    rows, width = grad.shape
    deep = right.shape[0]
    count = tokens.shape[0]
    part = count // nx
    per = nz // nx
    spans = chunks(width)

    def of_y(array, which, size):
        size *= 2
        return jnp.concatenate(
            [columns(array, (2 * i + which) * size, size) for i in range(per)], axis=1
        )

    share = lax.dynamic_slice_in_dim(tokens, x * part, part, 0)

    def piece(level):
        return jnp.concatenate(
            [
                columns(share, (level * 4 + (y ^ dy) * 2 + (k ^ dk)) * rows, rows)
                for dk in range(2)
                for dy in range(2)
            ],
            axis=1,
        )

    def gather_levels(block):
        return lax.all_gather(block, ("z", "k"), axis=0, tiled=True)

    def multiply_tokens(narrow, near):
        narrow = jnp.concatenate([narrow, near], axis=0)
        narrow = jnp.concatenate([narrow, swap(narrow, "k")], axis=0)
        sums = dot(token_panel, narrow)
        total = sums[:count]
        for by in range(1, nz):
            send = sums[by * count : (by + 1) * count].astype(BF16)
            total += shift(send, "z", nz, -by).astype(F32)
        return total.astype(BF16)

    half, upper = width // 2, rows // 2

    def multiply(borrowed, panel):
        return swap(dot(borrowed, panel).astype(BF16), "y")

    def cut(product, first):
        return [
            product[:, a - first : b - first]
            for a, b in spans
            if first <= a < first + half
        ]

    right_panel = gather_levels(right[:, :half])
    grad_mine = of_y(grad, y, deep)
    left_mine, left_lent = of_y(left, y, rows), of_y(left, 1 - y, rows)
    now = tie(
        {
            "grad": [grad_mine, *others(grad_mine, "x", nx)],
            "borrowed": swap(of_y(grad, 1 - y, deep), "y"),
            "right": right[:, half:],
            "lent": left_lent[:upper],
            "mine": [left_mine[:upper], left_mine[upper:]],
        }
    )
    mine = now["mine"]
    grad_mine = place(jnp.zeros((rows, nz * 2 * deep), BF16), now["grad"], x, 0)
    next_panel = gather_levels(now["right"])
    now = tie(
        {
            "grad": [now["borrowed"], *others(now["borrowed"], "x", nx)],
            "borrowed": swap(now["lent"], "y"),
            "lent": left_lent[upper:],
            "mine": mine[0],
        }
    )
    borrowed = [now["borrowed"]]
    grad_borrowed = place(jnp.zeros((rows, nz * 2 * deep), BF16), now["grad"], x, 0)
    now = tie(
        {
            "mine": [now["mine"], *others(now["mine"], "x", nx)],
            "received": multiply(grad_borrowed, right_panel),
            "grad": grad_borrowed,
            "lent": now["lent"],
            "next": mine[1],
        }
    )
    both = place(jnp.zeros((2 * rows, nz * 2 * rows), BF16), now["mine"], x, 0)
    grad_borrowed = now["grad"]
    product = (dot(grad_mine, right_panel) + now["received"].astype(F32)).astype(BF16)
    products = cut(product, 0)
    early = len(products)
    now = tie(
        {
            "mine": [now["next"], *others(now["next"], "x", nx)],
            "borrowed": swap(now["lent"], "y"),
            "first": borrowed[0],
            "products": products[1:],
            "spread": [piece((z + by) % nz) for by in range(nz)],
        }
    )
    both = place(both, now["mine"], x, upper)
    products[1:] = now["products"]
    panels = [gather_levels(products[0])]
    borrowed = [now["first"], now["borrowed"]]
    spread = now["spread"]
    now = tie(
        {
            "borrowed": [borrowed[0], *others(borrowed[0], "x", nx)],
            "next": borrowed[1],
            "received": multiply(grad_borrowed, next_panel),
            "spread": spread[:1]
            + [shift(spread[by], "z", nz, by) for by in range(1, nz)],
            "products": products[1:],
        }
    )
    both = place(both, now["borrowed"], x, rows)
    products[1:] = now["products"]
    product = (dot(grad_mine, next_panel) + now["received"].astype(F32)).astype(BF16)
    products += cut(product, half)
    now = tie(
        {
            "borrowed": [now["next"], *others(now["next"], "x", nx)],
            "products": products[early:],
            "spread": now["spread"],
        }
    )
    both = place(both, now["borrowed"], x, rows + upper)
    products[early:] = now["products"]
    spread = jnp.concatenate(now["spread"], axis=0)
    spread = [
        block.reshape(nz, part, 4 * rows) for block in [spread, *others(spread, "x", nx)]
    ]
    token_panel = jnp.zeros((nz, count, 4 * rows), BF16)
    for by, block in enumerate(spread):
        token_panel = lax.dynamic_update_slice(
            token_panel, block, (0, (x + by) % nx * part, 0)
        )
    token_panel = token_panel.reshape(nz * count, 4 * rows)

    def updated(span, precond):
        nonlocal new_weight
        start, stop = span
        update = weight[:, start:stop] - 0.01 * precond
        new_weight = lax.dynamic_update_slice(new_weight, update, (0, start))
        narrow = update.astype(BF16)
        return narrow, swap(narrow, "y")

    new_weight, outputs, previous = weight, [], None
    for i, (span, product) in enumerate(zip(spans, products)):
        panel = gather_levels(product) if i else panels[0]
        if previous is not None:
            panel, previous, outputs = tie((panel, previous, outputs))
            outputs.append(multiply_tokens(*previous))
        received = swap(dot(both[rows:], panel).astype(BF16), "y")
        previous = updated(span, dot(both[:rows], panel) + received.astype(F32))
    previous, outputs = tie((previous, outputs))
    outputs.append(multiply_tokens(*previous))
    return new_weight, jnp.concatenate(outputs, axis=1)


def solution(mesh):
    nrow, ncol = mesh.shape["row"], mesh.shape["col"]
    sizes = {"z": nrow // 4, "y": 2, "k": 2, "x": ncol}
    fine = Mesh(mesh.devices.reshape(nrow // 4, 2, 2, ncol), ("z", "y", "k", "x"))
    split = P(ROWS, "x")
    return jax.shard_map(
        lambda *args: step(sizes, *args),
        mesh=fine,
        in_specs=(split, split, split, split, P(ROWS, None)),
        out_specs=(split, split),
        check_vma=False,
    )
```

time: 430 us -> 398 us (0.926)
  waiting for transfers between devices: 248 us -> 178 us
  local copies, waits for them, and re-layouts: 18.9 us -> 47.4 us
  starting transfers between devices: 45 us -> 67.4 us
  other arithmetic: 29.4 us -> 12.2 us
    ppermute x38 -> x39, waiting for transfers between devices: 219 us -> 178 us  [shift(): lax.ppermute(block, axis, [(i, (i + by) % size) for i in range(size)])]
    all_gather x6, waiting for transfers between devices: 28.9 us -> 0.03 us  [gather_levels(): return lax.all_gather(block, ('z', 'k'), axis=0, tiled=True)]
    ppermute x38 -> x39, starting transfers between devices: 44.6 us -> 67 us  [shift(): lax.ppermute(block, axis, [(i, (i + by) % size) for i in range(size)])]
    dynamic_update_slice x0 -> x14, local copies, waits for them, and re-layouts: none -> 15.9 us  [the longest x12 13 us: place(): whole = lax.dynamic_update_slice(whole, block, (row, column))]
    select_n x5 -> x0, other arithmetic: 10.3 us -> none  [lay(): first, last = (jnp.where(me == 0, a, b), jnp.where(me == 0, b, a))]
    unnamed x119 -> x102, local copies, waits for them, and re-layouts: 8.06 us -> 15.2 us
    broadcast_in_dim x0 -> x2, local copies, waits for them, and re-layouts: none -> 4.63 us  [the longest x1 4.39 us: step(): both = place(jnp.zeros((2 * rows, nz * 2 * rows), BF16), now['mine'], x, 0)]
    dot_general x20 -> x16, matrix products: 74.1 us -> 77.9 us  [dot(): return jnp.dot(a, b, preferred_element_type=F32)]
  transfers between devices with their start and end apart: 44 -> 45, of which waited for: 23 -> 26; matrix products, arithmetic and copies ran while one was open for 27% -> 30% of each run, Pallas kernels for 0% -> 0%
where the time goes in v2:
time: 398 us
  waiting for transfers between devices  178 us (45%)
  matrix products  77.9 us (20%)
  starting transfers between devices  67.4 us (17%)
  local copies, waits for them, and re-layouts  47.4 us (12%)
  between operations  15 us (4%)
  other arithmetic  12.2 us (3%)
    ppermute x39, waiting for transfers between devices, shift(): lax.ppermute(block, axis, [(i, (i + by) % size) for i in range(size)])  178 us
    dot_general x16, matrix products, dot(): return jnp.dot(a, b, preferred_element_type=F32)  77.9 us
    ppermute x39, starting transfers between devices, shift(): lax.ppermute(block, axis, [(i, (i + by) % size) for i in range(size)])  67 us
    unnamed x102, local copies, waits for them, and re-layouts  15.2 us
    dynamic_update_slice x12, local copies, waits for them, and re-layouts, place(): whole = lax.dynamic_update_slice(whole, block, (row, column))  13 us
  transfers between devices with their start and end apart: 45, of which 26 were waited for; matrix products, arithmetic and copies ran while one was open for 30% of the time, Pallas kernels for 0%

profile of v2, /device:TPU:0, one launch (start us, length us, event | category | flops | bytes accessed | tf_op | source)
XLA Modules:
  0.0 398.1 jit_solution(3784723695263436135)
XLA Ops:
  20.7 15.5 %collective-permute-done.1.refs_2_ = bf16[512,1024]{1,0:T(8,128)(2,1)S(1)} collective-permute-done((bf16[512,1024]{1,0:T(8,128)(2,1)S(1)}, bf16[512,1024]{1,0:T(8,128)(2,1)S(1)}, u32[]{:S(2)}, u32[]{:S(2)}) %collective-permute-start.1) | collective-permute-done | bytes 1048608 | tf_op jit(solution)/shard_map/ppermute | solution.py:14
  42.2 22.0 %collective-permute-done.2.refs_0_ = bf16[256,2048]{1,0:T(8,128)(2,1)S(1)} collective-permute-done((bf16[256,2048]{1,0:T(8,128)(2,1)}, bf16[256,2048]{1,0:T(8,128)(2,1)S(1)}, u32[]{:S(2)}, u32[]{:S(2)}) %collective-permute-start.2) | collective-permute-done | bytes 1048608 | tf_op jit(solution)/shard_map/ppermute | solution.py:14
  68.8 5.3 %convolution_convert_fusion.1 = bf16[512,1024]{1,0:T(8,128)(2,1)S(1)} fusion(bf16[512,2048]{1,0:T(8,128)(2,1)S(1)} %constant_dynamic-update-slice_fusion.14.refs_0_, bf16[2048,1024]{1,0:T(8,128)(2,1)} %all-gather.7.cloned.1.call-done), kind=kOutput, calls=%fused_computation.47 | convolution fusion | flops 2148007936 | bytes 7340032 | tf_op jit(solution)/shard_map/dot_general | solution.py:26
  75.5 13.8 %collective-permute-done.4.refs_3_ = bf16[256,2048]{1,0:T(8,128)(2,1)} collective-permute-done((bf16[256,2048]{1,0:T(8,128)(2,1)}, bf16[256,2048]{1,0:T(8,128)(2,1)}, u32[]{:S(2)}, u32[]{:S(2)}) %collective-permute-start.4) | collective-permute-done | bytes 1048608 | tf_op jit(solution)/shard_map/ppermute | solution.py:14
  89.3 7.5 %collective-permute-done.5.refs_5_ = bf16[512,1024]{1,0:T(8,128)(2,1)} collective-permute-done((bf16[512,1024]{1,0:T(8,128)(2,1)S(1)}, bf16[512,1024]{1,0:T(8,128)(2,1)}, u32[]{:S(2)}, u32[]{:S(2)}) %collective-permute-start.5) | collective-permute-done | bytes 1048608 | tf_op jit(solution)/shard_map/ppermute | solution.py:14
  96.8 4.8 %add_convert_fusion.1 = bf16[512,1024]{1,0:T(8,128)(2,1)S(1)} fusion(bf16[512,1024]{1,0:T(8,128)(2,1)} %get-tuple-element.78, bf16[512,2048]{1,0:T(8,128)(2,1)S(1)} %constant_dynamic-update-slice_fusion.10, bf16[2048,1024]{1,0:T(8,128)(2,1)} %all-gather.7.cloned.1.call-done), kind=kOutput, calls=%fused_computation.39 | convolution fusion | flops 2149056512 | bytes 8388608 | tf_op jit(solution)/shard_map/dot_general | solution.py:26
  109.3 6.1 %convolution_convert_fusion = bf16[512,1024]{1,0:T(8,128)(2,1)} fusion(bf16[512,2048]{1,0:T(8,128)(2,1)} %get-tuple-element.84, bf16[2048,1024]{1,0:T(8,128)(2,1)} %all-gather.9.cloned.1.call-done), kind=kOutput, calls=%fused_computation.46 | convolution fusion | flops 2148007936 | bytes 7340032 | tf_op jit(solution)/shard_map/dot_general | solution.py:26
  116.7 14.8 %collective-permute-done.6.refs_0_ = bf16[256,2048]{1,0:T(8,128)(2,1)S(1)} collective-permute-done((bf16[256,2048]{1,0:T(8,128)(2,1)S(1)}, bf16[256,2048]{1,0:T(8,128)(2,1)S(1)}, u32[]{:S(2)}, u32[]{:S(2)}) %collective-permute-start.6) | collective-permute-done | bytes 1048608 | tf_op jit(solution)/shard_map/ppermute | solution.py:14
  139.4 10.1 %collective-permute-done.9.refs_4_ = bf16[512,1024]{1,0:T(8,128)(2,1)} collective-permute-done((bf16[512,1024]{1,0:T(8,128)(2,1)}, bf16[512,1024]{1,0:T(8,128)(2,1)}, u32[]{:S(2)}, u32[]{:S(2)}) %collective-permute-start.9) | collective-permute-done | bytes 1048608 | tf_op jit(solution)/shard_map/ppermute | solution.py:14
  150.7 15.1 %collective-permute-done.11.refs_7_ = bf16[64,2048]{1,0:T(8,128)(2,1)S(1)} collective-permute-done((bf16[64,2048]{1,0:T(8,128)(2,1)}, bf16[64,2048]{1,0:T(8,128)(2,1)S(1)}, u32[]{:S(2)}, u32[]{:S(2)}) %collective-permute-start.11) | collective-permute-done | bytes 262176 | tf_op jit(solution)/shard_map/ppermute | solution.py:14
  169.1 5.5 %add_convert_fusion = bf16[512,1024]{1,0:T(8,128)(2,1)S(1)} fusion(bf16[512,1024]{1,0:T(8,128)(2,1)} %get-tuple-element.93, bf16[512,2048]{1,0:T(8,128)(2,1)} %copy-done.37, bf16[2048,1024]{1,0:T(8,128)(2,1)} %all-gather.9.cloned.1.call-done), kind=kOutput, calls=%fused_computation.38 | convolution fusion | flops 2149056512 | bytes 8388608 | tf_op jit(solution)/shard_map/dot_general | solution.py:26
  176.3 8.1 %collective-permute-done.13.refs_1_ = bf16[256,2048]{1,0:T(8,128)(2,1)S(1)} collective-permute-done((bf16[256,2048]{1,0:T(8,128)(2,1)}, bf16[256,2048]{1,0:T(8,128)(2,1)S(1)}, u32[]{:S(2)}, u32[]{:S(2)}) %collective-permute-start.13) | collective-permute-done | bytes 1048608 | tf_op jit(solution)/shard_map/ppermute | solution.py:14
  185.4 4.4 %broadcast_in_dim.6 = bf16[1024,4096]{1,0:T(8,128)(2,1)} broadcast(bf16[]{:T(256)} %constant.249.clone.1), dimensions={} | broadcast | bytes 8388610 | tf_op jit(solution)/shard_map/broadcast_in_dim | solution.py:146
  201.0 5.8 %fusion.70 = bf16[512,512]{1,0:T(8,128)(2,1)S(1)} fusion(bf16[4096,512]{1,0:T(8,128)(2,1)} %all-gather.11.cloned.1.call-done, bf16[1024,4096]{1,0:T(8,128)(2,1)} %constant_dynamic-update-slice_fusion.16), kind=kOutput, calls=%fused_computation.59 | convolution fusion | flops 2147745792 | bytes 8912896 | tf_op jit(solution)/shard_map/dot_general | solution.py:26
  208.7 4.8 %copy.127 = f32[512,2048]{1,0:T(8,128)} copy(f32[512,2048]{1,0:T(8,128)} %param.5) | data formatting | bytes 8388608
  216.1 6.1 %fusion.67 = f32[512,512]{1,0:T(8,128)S(1)} fusion(bf16[4096,512]{1,0:T(8,128)(2,1)} %all-gather.11.cloned.1.call-done, bf16[1024,4096]{1,0:T(8,128)(2,1)} %constant_dynamic-update-slice_fusion.16, bf16[512,512]{1,0:T(8,128)(2,1)S(1)} %collective-permute-done.14, f32[512,2048]{1,0:T(8,128)} %param.5), kind=kOutput, calls=%fused_computation.58 | convolution fusion | flops 2148532224 | bytes 11010048 | tf_op jit(solution)/shard_map/dot_general | solution.py:26
  233.4 5.9 %fusion.73 = bf16[512,512]{1,0:T(8,128)(2,1)S(1)} fusion(bf16[4096,512]{1,0:T(8,128)(2,1)} %get-tuple-element.101, bf16[1024,4096]{1,0:T(8,128)(2,1)} %constant_dynamic-update-slice_fusion.16), kind=kOutput, calls=%fused_computation.60 | convolution fusion | flops 2147745792 | bytes 8912896 | tf_op jit(solution)/shard_map/dot_general | solution.py:26
  244.4 4.1 %collective-permute-done.16 = bf16[512,512]{1,0:T(8,128)(2,1)S(1)} collective-permute-done((bf16[512,512]{1,0:T(8,128)(2,1)S(1)}, bf16[512,512]{1,0:T(8,128)(2,1)S(1)}, u32[]{:S(2)}, u32[]{:S(2)}) %collective-permute-start.16) | collective-permute-done | bytes 524320 | tf_op jit(solution)/shard_map/ppermute | solution.py:14
  248.5 5.9 %fusion.108 = (bf16[512,512]{1,0:T(8,128)(2,1)S(1)}, f32[512,2048]{1,0:T(8,128)}) fusion(f32[512,2048]{1,0:T(8,128)} %get-tuple-element.157, bf16[512,512]{1,0:T(8,128)(2,1)S(1)} %collective-permute-done.16, bf16[4096,512]{1,0:T(8,128)(2,1)S(1)} %copy-done.18, bf16[1024,4096]{1,0:T(8,128)(2,1)} %constant_dynamic-update-slice_fusion.16, f32[512,2048]{1,0:T(8,128)} %param.5), kind=kOutput, calls=%fused_computation.131 | convolution fusion | flops 2148794368 | bytes 11534336 | tf_op jit(solution)/shard_map/dot_general | solution.py:26
  257.4 18.0 %collective-permute-start.20 = (bf16[128,512]{1,0:T(8,128)(2,1)S(1)}, bf16[128,512]{1,0:T(8,128)(2,1)S(1)}, u32[]{:S(2)}, u32[]{:S(2)}) collective-permute-start(bf16[128,512]{1,0:T(8,128)(2,1)S(1)} %get-tuple-element.170), channel_id=1, source_target_pairs={{0,24},{8,0},{16,8},{24,16},{1,25},{9,1},{17,9},{25,17},{2,26},{10... | collective-permute-start | bytes 393224 | tf_op jit(solution)/shard_map/ppermute | solution.py:14
  275.4 5.4 %collective-permute-start.21 = (bf16[128,512]{1,0:T(8,128)(2,1)S(1)}, bf16[128,512]{1,0:T(8,128)(2,1)S(1)}, u32[]{:S(2)}, u32[]{:S(2)}) collective-permute-start(bf16[128,512]{1,0:T(8,128)(2,1)S(1)} %get-tuple-element.172), channel_id=1, source_target_pairs={{0,16},{8,24},{16,0},{24,8},{1,17},{9,25},{17,1},{25,9},{2,18},{10... | collective-permute-start | bytes 393224 | tf_op jit(solution)/shard_map/ppermute | solution.py:14
  283.7 6.6 %collective-permute-done.21 = bf16[128,512]{1,0:T(8,128)(2,1)S(1)} collective-permute-done((bf16[128,512]{1,0:T(8,128)(2,1)S(1)}, bf16[128,512]{1,0:T(8,128)(2,1)S(1)}, u32[]{:S(2)}, u32[]{:S(2)}) %collective-permute-start.21) | collective-permute-done | bytes 131104 | tf_op jit(solution)/shard_map/ppermute | solution.py:14
  291.8 7.4 %fusion.49 = bf16[512,640]{1,0:T(8,128)(2,1)S(1)} fusion(bf16[4096,640]{1,0:T(8,128)(2,1)} %get-tuple-element.109, bf16[1024,4096]{1,0:T(8,128)(2,1)} %constant_dynamic-update-slice_fusion.16), kind=kOutput, calls=%fused_computation.51 | convolution fusion | flops 2684682240 | bytes 10092544 | tf_op jit(solution)/shard_map/dot_general | solution.py:26
  300.8 13.6 %collective-permute-done.23 = bf16[512,640]{1,0:T(8,128)(2,1)S(1)} collective-permute-done((bf16[512,640]{1,0:T(8,128)(2,1)S(1)}, bf16[512,640]{1,0:T(8,128)(2,1)S(1)}, u32[]{:S(2)}, u32[]{:S(2)}) %collective-permute-start.23) | collective-permute-done | bytes 655392 | tf_op jit(solution)/shard_map/ppermute | solution.py:14
  314.4 7.1 %fusion.107 = (bf16[512,640]{1,0:T(8,128)(2,1)S(1)}, f32[512,2048]{1,0:T(8,128)}) fusion(f32[512,2048]{1,0:T(8,128)} %get-tuple-element.155, bf16[512,640]{1,0:T(8,128)(2,1)S(1)} %collective-permute-done.23, bf16[4096,640]{1,0:T(8,128)(2,1)S(1)} %copy-done.13, bf16[1024,4096]{1,0:T(8,128)(2,1)} %constant_dynamic-update-slice_fusion.16, f32[512,2048]{1,0:T(8,128)} %param.5), kind=kOutput, calls=%fused_computation.130 | convolution fusion | flops 2685992960 | bytes 13369344 | tf_op jit(solution)/shard_map/dot_general | solution.py:26
  327.6 3.7 collective-permute-done.26
  331.3 5.2 %collective-permute-done.27 = bf16[128,512]{1,0:T(8,128)(2,1)S(1)} collective-permute-done((bf16[128,512]{1,0:T(8,128)(2,1)S(1)}, bf16[128,512]{1,0:T(8,128)(2,1)S(1)}, u32[]{:S(2)}, u32[]{:S(2)}) %collective-permute-start.27) | collective-permute-done | bytes 131104 | tf_op jit(solution)/shard_map/ppermute | solution.py:14
  339.5 5.6 %fusion.85 = bf16[512,384]{1,0:T(8,128)(2,1)S(1)} fusion(bf16[4096,384]{1,0:T(8,128)(2,1)} %get-tuple-element.114, bf16[1024,4096]{1,0:T(8,128)(2,1)} %constant_dynamic-update-slice_fusion.16), kind=kOutput, calls=%fused_computation.64 | convolution fusion | flops 1610809344 | bytes 7733248 | tf_op jit(solution)/shard_map/dot_general | solution.py:26
  351.6 5.1 %collective-permute-done.29 = bf16[512,384]{1,0:T(8,128)(2,1)S(1)} collective-permute-done((bf16[512,384]{1,0:T(8,128)(2,1)S(1)}, bf16[512,384]{1,0:T(8,128)(2,1)S(1)}, u32[]{:S(2)}, u32[]{:S(2)}) %collective-permute-start.29) | collective-permute-done | bytes 393248 | tf_op jit(solution)/shard_map/ppermute | solution.py:14
  356.7 5.7 %fusion.112 = (bf16[512,384]{1,0:T(8,128)(2,1)S(1)}, f32[512,2048]{1,0:T(8,128)}) fusion(f32[512,2048]{1,0:T(8,128)} %get-tuple-element.153, bf16[512,384]{1,0:T(8,128)(2,1)S(1)} %collective-permute-done.29, bf16[4096,384]{1,0:T(8,128)(2,1)S(1)} %copy-done.26, bf16[1024,4096]{1,0:T(8,128)(2,1)} %constant_dynamic-update-slice_fusion.16, f32[512,2048]{1,0:T(8,128)} %param.5), kind=kOutput, calls=%fused_computation.135 | convolution fusion | flops 1611595776 | bytes 9699328 | tf_op jit(solution)/shard_map/dot_general | solution.py:26
  365.4 7.7 %collective-permute-done.30.refs_1_ = bf16[512,384]{1,0:T(8,128)(2,1)S(1)} collective-permute-done((bf16[512,384]{1,0:T(8,128)(2,1)S(1)}, bf16[512,384]{1,0:T(8,128)(2,1)S(1)}, u32[]{:S(2)}, u32[]{:S(2)}) %collective-permute-start.30) | collective-permute-done | bytes 393248 | tf_op jit(solution)/shard_map/ppermute | solution.py:14
  385.9 4.4 %collective-permute-done.37 = bf16[128,384]{1,0:T(8,128)(2,1)S(1)} collective-permute-done((bf16[128,384]{1,0:T(8,128)(2,1)S(1)}, bf16[128,384]{1,0:T(8,128)(2,1)S(1)}, u32[]{:S(2)}, u32[]{:S(2)}) %collective-permute-start.37) | collective-permute-done | bytes 98336 | tf_op jit(solution)/shard_map/ppermute | solution.py:14
  (237 shorter events, 122.2 us)
Async XLA Ops:
  7.2 61.6 %all-gather.7.cloned.1.call-start = ((), (), s32[]{:S(2)}) async-start(), calls=%async_computation | async-start | bytes 4718592 | tf_op jit(solution)/shard_map/all_gather | solution.py:88
  9.6 99.7 %all-gather.9.cloned.1.call-start = ((), (), s32[]{:S(2)}) async-start(), calls=%async_computation.1 | async-start | bytes 4718592 | tf_op jit(solution)/shard_map/all_gather | solution.py:88
  10.1 26.2 %collective-permute-start.1 = (bf16[512,1024]{1,0:T(8,128)(2,1)S(1)}, bf16[512,1024]{1,0:T(8,128)(2,1)S(1)}, u32[]{:S(2)}, u32[]{:S(2)}) collective-permute-start(bf16[512,1024]{1,0:T(8,128)(2,1)S(1)} %pad_maximum_fusion.4.refs_1_), channel_id=1, source_target_pairs={{0,1},{1,0},{2,3},{3,2},{4,5},{5,4},{6,7},{7,6},{8,9},{9,8},{10,11... | collective-permute-start | bytes 3145736 | tf_op jit(solution)/shard_map/ppermute | solution.py:14
  14.2 24.8 %collective-permute-start = (bf16[512,1024]{1,0:T(8,128)(2,1)}, bf16[512,1024]{1,0:T(8,128)(2,1)S(1)}, u32[]{:S(2)}, u32[]{:S(2)}) collective-permute-start(bf16[512,1024]{1,0:T(8,128)(2,1)} %pad_maximum_fusion.3), channel_id=1, source_target_pairs={{0,4},{4,0},{1,5},{5,1},{2,6},{6,2},{3,7},{7,3},{8,12},{12,8},{9,1... | collective-permute-start | bytes 3145736 | tf_op jit(solution)/shard_map/ppermute | solution.py:14
  40.0 161.0 %all-gather.11.cloned.1.call-start = ((), (), s32[]{:S(2)}) async-start(), calls=%async_computation.2 | async-start | bytes 4718592 | tf_op jit(solution)/shard_map/all_gather | solution.py:88
  40.1 24.1 %collective-permute-start.2 = (bf16[256,2048]{1,0:T(8,128)(2,1)}, bf16[256,2048]{1,0:T(8,128)(2,1)S(1)}, u32[]{:S(2)}, u32[]{:S(2)}) collective-permute-start(bf16[256,2048]{1,0:T(8,128)(2,1)} %get-tuple-element.63), channel_id=1, source_target_pairs={{0,4},{4,0},{1,5},{5,1},{2,6},{6,2},{3,7},{7,3},{8,12},{12,8},{9,1... | collective-permute-start | bytes 3145736 | tf_op jit(solution)/shard_map/ppermute | solution.py:14
  41.6 23.7 %collective-permute-start.3 = (bf16[512,1024]{1,0:T(8,128)(2,1)}, bf16[512,1024]{1,0:T(8,128)(2,1)S(1)}, u32[]{:S(2)}, u32[]{:S(2)}) collective-permute-start(bf16[512,1024]{1,0:T(8,128)(2,1)} %get-tuple-element.64.refs_1_), channel_id=1, source_target_pairs={{0,1},{1,0},{2,3},{3,2},{4,5},{5,4},{6,7},{7,6},{8,9},{9,8},{10,11... | collective-permute-start | bytes 3145736 | tf_op jit(solution)/shard_map/ppermute | solution.py:14
  66.4 22.9 %collective-permute-start.4 = (bf16[256,2048]{1,0:T(8,128)(2,1)}, bf16[256,2048]{1,0:T(8,128)(2,1)}, u32[]{:S(2)}, u32[]{:S(2)}) collective-permute-start(bf16[256,2048]{1,0:T(8,128)(2,1)} %get-tuple-element.69.refs_2_), channel_id=1, source_target_pairs={{0,1},{1,0},{2,3},{3,2},{4,5},{5,4},{6,7},{7,6},{8,9},{9,8},{10,11... | collective-permute-start | bytes 3145736 | tf_op jit(solution)/shard_map/ppermute | solution.py:14
  74.1 22.6 %collective-permute-start.5 = (bf16[512,1024]{1,0:T(8,128)(2,1)S(1)}, bf16[512,1024]{1,0:T(8,128)(2,1)}, u32[]{:S(2)}, u32[]{:S(2)}) collective-permute-start(bf16[512,1024]{1,0:T(8,128)(2,1)S(1)} %convolution_convert_fusion.1), channel_id=1, source_target_pairs={{0,4},{4,0},{1,5},{5,1},{2,6},{6,2},{3,7},{7,3},{8,12},{12,8},{9,1... | collective-permute-start | bytes 3145736 | tf_op jit(solution)/shard_map/ppermute | solution.py:14
  102.8 129.8 %all-gather.13.cloned.1.call-start = ((), (), s32[]{:S(2)}) async-start(), calls=%async_computation.3 | async-start | bytes 4718592 | tf_op jit(solution)/shard_map/all_gather | solution.py:88
  105.3 26.2 %collective-permute-start.6 = (bf16[256,2048]{1,0:T(8,128)(2,1)S(1)}, bf16[256,2048]{1,0:T(8,128)(2,1)S(1)}, u32[]{:S(2)}, u32[]{:S(2)}) collective-permute-start(bf16[256,2048]{1,0:T(8,128)(2,1)S(1)} %copy-done.8), channel_id=1, source_target_pairs={{0,4},{4,0},{1,5},{5,1},{2,6},{6,2},{3,7},{7,3},{8,12},{12,8},{9,1... | collective-permute-start | bytes 3145736 | tf_op jit(solution)/shard_map/ppermute | solution.py:14
  106.4 25.1 %collective-permute-start.7 = (bf16[256,2048]{1,0:T(8,128)(2,1)S(1)}, bf16[256,2048]{1,0:T(8,128)(2,1)}, u32[]{:S(2)}, u32[]{:S(2)}) collective-permute-start(bf16[256,2048]{1,0:T(8,128)(2,1)S(1)} %copy-done.1), channel_id=1, source_target_pairs={{0,1},{1,0},{2,3},{3,2},{4,5},{5,4},{6,7},{7,6},{8,9},{9,8},{10,11... | collective-permute-start | bytes 3145736 | tf_op jit(solution)/shard_map/ppermute | solution.py:14
  115.5 34.0 %collective-permute-start.9 = (bf16[512,1024]{1,0:T(8,128)(2,1)}, bf16[512,1024]{1,0:T(8,128)(2,1)}, u32[]{:S(2)}, u32[]{:S(2)}) collective-permute-start(bf16[512,1024]{1,0:T(8,128)(2,1)} %convolution_convert_fusion), channel_id=1, source_target_pairs={{0,4},{4,0},{1,5},{5,1},{2,6},{6,2},{3,7},{7,3},{8,12},{12,8},{9,1... | collective-permute-start | bytes 3145736 | tf_op jit(solution)/shard_map/ppermute | solution.py:14
  132.4 34.5 %collective-permute-start.8 = (bf16[256,2048]{1,0:T(8,128)(2,1)}, bf16[256,2048]{1,0:T(8,128)(2,1)S(1)}, u32[]{:S(2)}, u32[]{:S(2)}) collective-permute-start(bf16[256,2048]{1,0:T(8,128)(2,1)} %get-tuple-element.81.refs_0_), channel_id=1, source_target_pairs={{0,1},{1,0},{2,3},{3,2},{4,5},{5,4},{6,7},{7,6},{8,9},{9,8},{10,11... | collective-permute-start | bytes 3145736 | tf_op jit(solution)/shard_map/ppermute | solution.py:14
  133.9 16.8 %collective-permute-start.10 = (bf16[64,2048]{1,0:T(8,128)(2,1)}, bf16[64,2048]{1,0:T(8,128)(2,1)S(1)}, u32[]{:S(2)}, u32[]{:S(2)}) collective-permute-start(bf16[64,2048]{1,0:T(8,128)(2,1)} %get-tuple-element.87), channel_id=1, source_target_pairs={{0,8},{8,16},{16,24},{24,0},{1,9},{9,17},{17,25},{25,1},{2,10},{10... | collective-permute-start | bytes 786440 | tf_op jit(solution)/shard_map/ppermute | solution.py:14
  135.2 30.6 %collective-permute-start.11 = (bf16[64,2048]{1,0:T(8,128)(2,1)}, bf16[64,2048]{1,0:T(8,128)(2,1)S(1)}, u32[]{:S(2)}, u32[]{:S(2)}) collective-permute-start(bf16[64,2048]{1,0:T(8,128)(2,1)} %get-tuple-element.88), channel_id=1, source_target_pairs={{0,16},{8,24},{16,0},{24,8},{1,17},{9,25},{17,1},{25,9},{2,18},{10... | collective-permute-start | bytes 786440 | tf_op jit(solution)/shard_map/ppermute | solution.py:14
  138.1 28.8 %collective-permute-start.12 = (bf16[64,2048]{1,0:T(8,128)(2,1)}, bf16[64,2048]{1,0:T(8,128)(2,1)S(1)}, u32[]{:S(2)}, u32[]{:S(2)}) collective-permute-start(bf16[64,2048]{1,0:T(8,128)(2,1)} %get-tuple-element.89), channel_id=1, source_target_pairs={{0,24},{8,0},{16,8},{24,16},{1,25},{9,1},{17,9},{25,17},{2,26},{10... | collective-permute-start | bytes 786440 | tf_op jit(solution)/shard_map/ppermute | solution.py:14
  168.0 123.0 %all-gather.15.cloned.1.call-start = ((), (), s32[]{:S(2)}) async-start(), calls=%async_computation.4 | async-start | bytes 5898240 | tf_op jit(solution)/shard_map/all_gather | solution.py:88
  168.2 16.1 %collective-permute-start.13 = (bf16[256,2048]{1,0:T(8,128)(2,1)}, bf16[256,2048]{1,0:T(8,128)(2,1)S(1)}, u32[]{:S(2)}, u32[]{:S(2)}) collective-permute-start(bf16[256,2048]{1,0:T(8,128)(2,1)} %get-tuple-element.92.refs_0_), channel_id=1, source_target_pairs={{0,1},{1,0},{2,3},{3,2},{4,5},{5,4},{6,7},{7,6},{8,9},{9,8},{10,11... | collective-permute-start | bytes 3145736 | tf_op jit(solution)/shard_map/ppermute | solution.py:14
  185.3 151.9 %all-gather.17.cloned.1.call-start = ((), (), s32[]{:S(2)}) async-start(), calls=%async_computation.5 | async-start | bytes 3538944 | tf_op jit(solution)/shard_map/all_gather | solution.py:88
  227.3 15.8 %collective-permute-start.18 = (bf16[256,2048]{1,0:T(8,128)(2,1)}, bf16[256,2048]{1,0:T(8,128)(2,1)}, u32[]{:S(2)}, u32[]{:S(2)}) collective-permute-start(bf16[256,2048]{1,0:T(8,128)(2,1)} %constant_dynamic-update-slice_fusion), channel_id=1, source_target_pairs={{0,1},{1,0},{2,3},{3,2},{4,5},{5,4},{6,7},{7,6},{8,9},{9,8},{10,11... | collective-permute-start | bytes 3145736 | tf_op jit(solution)/shard_map/ppermute | solution.py:14
  241.1 15.0 %collective-permute-start.19 = (bf16[1024,512]{1,0:T(8,128)(2,1)S(1)}, bf16[1024,512]{1,0:T(8,128)(2,1)S(1)}, u32[]{:S(2)}, u32[]{:S(2)}) collective-permute-start(bf16[1024,512]{1,0:T(8,128)(2,1)S(1)} %pad_maximum_fusion.5), channel_id=1, source_target_pairs={{0,2},{2,0},{1,3},{3,1},{4,6},{6,4},{5,7},{7,5},{8,10},{10,8},{9,1... | collective-permute-start | bytes 3145736 | tf_op jit(solution)/shard_map/ppermute | solution.py:14
  254.4 36.6 %collective-permute-start.17 = (bf16[512,512]{1,0:T(8,128)(2,1)S(1)}, bf16[512,512]{1,0:T(8,128)(2,1)S(1)}, u32[]{:S(2)}, u32[]{:S(2)}) collective-permute-start(bf16[512,512]{1,0:T(8,128)(2,1)S(1)} %get-tuple-element.154.refs_1_), channel_id=1, source_target_pairs={{0,4},{4,0},{1,5},{5,1},{2,6},{6,2},{3,7},{7,3},{8,12},{12,8},{9,1... | collective-permute-start | bytes 1572872 | tf_op jit(solution)/shard_map/ppermute | solution.py:14
  257.4 26.3 %collective-permute-start.20 = (bf16[128,512]{1,0:T(8,128)(2,1)S(1)}, bf16[128,512]{1,0:T(8,128)(2,1)S(1)}, u32[]{:S(2)}, u32[]{:S(2)}) collective-permute-start(bf16[128,512]{1,0:T(8,128)(2,1)S(1)} %get-tuple-element.170), channel_id=1, source_target_pairs={{0,24},{8,0},{16,8},{24,16},{1,25},{9,1},{17,9},{25,17},{2,26},{10... | collective-permute-start | bytes 393224 | tf_op jit(solution)/shard_map/ppermute | solution.py:14
  275.4 14.8 %collective-permute-start.21 = (bf16[128,512]{1,0:T(8,128)(2,1)S(1)}, bf16[128,512]{1,0:T(8,128)(2,1)S(1)}, u32[]{:S(2)}, u32[]{:S(2)}) collective-permute-start(bf16[128,512]{1,0:T(8,128)(2,1)S(1)} %get-tuple-element.172), channel_id=1, source_target_pairs={{0,16},{8,24},{16,0},{24,8},{1,17},{9,25},{17,1},{25,9},{2,18},{10... | collective-permute-start | bytes 393224 | tf_op jit(solution)/shard_map/ppermute | solution.py:14
  299.2 15.2 %collective-permute-start.23 = (bf16[512,640]{1,0:T(8,128)(2,1)S(1)}, bf16[512,640]{1,0:T(8,128)(2,1)S(1)}, u32[]{:S(2)}, u32[]{:S(2)}) collective-permute-start(bf16[512,640]{1,0:T(8,128)(2,1)S(1)} %fusion.49), channel_id=1, source_target_pairs={{0,4},{4,0},{1,5},{5,1},{2,6},{6,2},{3,7},{7,3},{8,12},{12,8},{9,1... | collective-permute-start | bytes 1966088 | tf_op jit(solution)/shard_map/ppermute | solution.py:14
  300.8 22.6 %collective-permute-start.25 = (bf16[1024,512]{1,0:T(8,128)(2,1)S(1)}, bf16[1024,512]{1,0:T(8,128)(2,1)S(1)}, u32[]{:S(2)}, u32[]{:S(2)}) collective-permute-start(bf16[1024,512]{1,0:T(8,128)(2,1)S(1)} %pad_maximum_fusion.6), channel_id=1, source_target_pairs={{0,2},{2,0},{1,3},{3,1},{4,6},{6,4},{5,7},{7,5},{8,10},{10,8},{9,1... | collective-permute-start | bytes 3145736 | tf_op jit(solution)/shard_map/ppermute | solution.py:14
  321.6 15.6 %collective-permute-start.24 = (bf16[512,640]{1,0:T(8,128)(2,1)S(1)}, bf16[512,640]{1,0:T(8,128)(2,1)S(1)}, u32[]{:S(2)}, u32[]{:S(2)}) collective-permute-start(bf16[512,640]{1,0:T(8,128)(2,1)S(1)} %get-tuple-element.152.refs_1_), channel_id=1, source_target_pairs={{0,4},{4,0},{1,5},{5,1},{2,6},{6,2},{3,7},{7,3},{8,12},{12,8},{9,1... | collective-permute-start | bytes 1966088 | tf_op jit(solution)/shard_map/ppermute | solution.py:14
  324.7 11.8 %collective-permute-start.27 = (bf16[128,512]{1,0:T(8,128)(2,1)S(1)}, bf16[128,512]{1,0:T(8,128)(2,1)S(1)}, u32[]{:S(2)}, u32[]{:S(2)}) collective-permute-start(bf16[128,512]{1,0:T(8,128)(2,1)S(1)} %get-tuple-element.169), channel_id=1, source_target_pairs={{0,16},{8,24},{16,0},{24,8},{1,17},{9,25},{17,1},{25,9},{2,18},{10... | collective-permute-start | bytes 393224 | tf_op jit(solution)/shard_map/ppermute | solution.py:14
  348.6 15.3 %collective-permute-start.32 = (bf16[128,640]{1,0:T(8,128)(2,1)S(1)}, bf16[128,640]{1,0:T(8,128)(2,1)S(1)}, u32[]{:S(2)}, u32[]{:S(2)}) collective-permute-start(bf16[128,640]{1,0:T(8,128)(2,1)S(1)} %get-tuple-element.164), channel_id=1, source_target_pairs={{0,24},{8,0},{16,8},{24,16},{1,25},{9,1},{17,9},{25,17},{2,26},{10... | collective-permute-start | bytes 491528 | tf_op jit(solution)/shard_map/ppermute | solution.py:14
  348.6 16.0 %collective-permute-start.33 = (bf16[128,640]{1,0:T(8,128)(2,1)S(1)}, bf16[128,640]{1,0:T(8,128)(2,1)S(1)}, u32[]{:S(2)}, u32[]{:S(2)}) collective-permute-start(bf16[128,640]{1,0:T(8,128)(2,1)S(1)} %get-tuple-element.166), channel_id=1, source_target_pairs={{0,16},{8,24},{16,0},{24,8},{1,17},{9,25},{17,1},{25,9},{2,18},{10... | collective-permute-start | bytes 491528 | tf_op jit(solution)/shard_map/ppermute | solution.py:14
  349.6 15.0 %collective-permute-start.34 = (bf16[128,640]{1,0:T(8,128)(2,1)S(1)}, bf16[128,640]{1,0:T(8,128)(2,1)S(1)}, u32[]{:S(2)}, u32[]{:S(2)}) collective-permute-start(bf16[128,640]{1,0:T(8,128)(2,1)S(1)} %get-tuple-element.165), channel_id=1, source_target_pairs={{0,8},{8,16},{16,24},{24,0},{1,9},{9,17},{17,25},{25,1},{2,10},{10... | collective-permute-start | bytes 491528 | tf_op jit(solution)/shard_map/ppermute | solution.py:14
  (62 other events, 408.9 us)
Sparse Core Ops, SparseCore 0:
  10.2 49.7 all-gather.6
  61.5 45.9 all-gather.8
  109.2 67.4 all-gather.10
  178.7 45.5 all-gather.12
  225.8 55.7 all-gather.14
  283.1 43.8 all-gather.16

commit v3 on v2

--- a/solution.py
+++ b/solution.py
@@ -117,11 +117,12 @@
             "grad": [grad_mine, *others(grad_mine, "x", nx)],
             "borrowed": swap(of_y(grad, 1 - y, deep), "y"),
             "right": right[:, half:],
+            "spread": [piece((z + by) % nz) for by in range(nz)],
             "lent": left_lent[:upper],
             "mine": [left_mine[:upper], left_mine[upper:]],
         }
     )
-    mine = now["mine"]
+    mine, spread = now["mine"], now["spread"]
     grad_mine = place(jnp.zeros((rows, nz * 2 * deep), BF16), now["grad"], x, 0)
     next_panel = gather_levels(now["right"])
     now = tie(
@@ -130,9 +131,11 @@
             "borrowed": swap(now["lent"], "y"),
             "lent": left_lent[upper:],
             "mine": mine[0],
-        }
-    )
-    borrowed = [now["borrowed"]]
+            "spread": spread[:1]
+            + [shift(spread[by], "z", nz, by) for by in range(1, nz)],
+        }
+    )
+    borrowed, spread = [now["borrowed"]], now["spread"]
     grad_borrowed = place(jnp.zeros((rows, nz * 2 * deep), BF16), now["grad"], x, 0)
     now = tie(
         {
@@ -154,21 +157,17 @@
             "borrowed": swap(now["lent"], "y"),
             "first": borrowed[0],
             "products": products[1:],
-            "spread": [piece((z + by) % nz) for by in range(nz)],
         }
     )
     both = place(both, now["mine"], x, upper)
     products[1:] = now["products"]
     panels = [gather_levels(products[0])]
     borrowed = [now["first"], now["borrowed"]]
-    spread = now["spread"]
     now = tie(
         {
             "borrowed": [borrowed[0], *others(borrowed[0], "x", nx)],
             "next": borrowed[1],
             "received": multiply(grad_borrowed, next_panel),
-            "spread": spread[:1]
-            + [shift(spread[by], "z", nz, by) for by in range(1, nz)],
             "products": products[1:],
         }
     )
@@ -180,12 +179,11 @@
         {
             "borrowed": [now["next"], *others(now["next"], "x", nx)],
             "products": products[early:],
-            "spread": now["spread"],
         }
     )
     both = place(both, now["borrowed"], x, rows + upper)
     products[early:] = now["products"]
-    spread = jnp.concatenate(now["spread"], axis=0)
+    spread = jnp.concatenate(spread, axis=0)
     spread = [
         block.reshape(nz, part, 4 * rows) for block in [spread, *others(spread, "x", nx)]
     ]

time: 398 us -> 397 us (level)
  starting transfers between devices: 67.4 us -> 54.8 us
  matrix products: 77.9 us -> 83.1 us
    ppermute x39, starting transfers between devices: 67 us -> 54.4 us  [shift(): lax.ppermute(block, axis, [(i, (i + by) % size) for i in range(size)])]
    all_gather x6, waiting for transfers between devices: 0.03 us -> 7.16 us  [gather_levels(): return lax.all_gather(block, ('z', 'k'), axis=0, tiled=True)]
    ppermute x39, waiting for transfers between devices: 178 us -> 171 us  [shift(): lax.ppermute(block, axis, [(i, (i + by) % size) for i in range(size)])]
    dot_general x16, matrix products: 77.9 us -> 83.1 us  [dot(): return jnp.dot(a, b, preferred_element_type=F32)]
    unnamed x102 -> x120, local copies, waits for them, and re-layouts: 15.2 us -> 17.2 us
  transfers between devices with their start and end apart: 45 -> 45, of which waited for: 26 -> 27; matrix products, arithmetic and copies ran while one was open for 30% -> 33% of each run, Pallas kernels for 0% -> 0%
where the time goes in v3:
time: 397 us; the launch traced here: 396 us
  waiting for transfers between devices  178 us (45%)
  matrix products  83.1 us (21%)
  starting transfers between devices  54.8 us (14%)
  local copies, waits for them, and re-layouts  50.8 us (13%)
  between operations  14.9 us (4%)
  other arithmetic  14 us (4%)
    ppermute x39, waiting for transfers between devices, shift(): lax.ppermute(block, axis, [(i, (i + by) % size) for i in range(size)])  171 us
    dot_general x16, matrix products, dot(): return jnp.dot(a, b, preferred_element_type=F32)  83.1 us
    ppermute x39, starting transfers between devices, shift(): lax.ppermute(block, axis, [(i, (i + by) % size) for i in range(size)])  54.4 us
    unnamed x120, local copies, waits for them, and re-layouts  17.2 us
    dynamic_update_slice x12, local copies, waits for them, and re-layouts, place(): whole = lax.dynamic_update_slice(whole, block, (row, column))  13.4 us
  transfers between devices with their start and end apart: 45, of which 27 were waited for; matrix products, arithmetic and copies ran while one was open for 33% of the time, Pallas kernels for 0%

profile of v3, /device:TPU:0, one launch (start us, length us, event | category | flops | bytes accessed | tf_op | source)
XLA Modules:
  0.0 396.1 jit_solution(11692120338987417994)
XLA Ops:
  25.8 10.5 %collective-permute-done.1.refs_2_ = bf16[512,1024]{1,0:T(8,128)(2,1)S(1)} collective-permute-done((bf16[512,1024]{1,0:T(8,128)(2,1)S(1)}, bf16[512,1024]{1,0:T(8,128)(2,1)S(1)}, u32[]{:S(2)}, u32[]{:S(2)}) %collective-permute-start.1) | collective-permute-done | bytes 1048608 | tf_op jit(solution)/shard_map/ppermute | solution.py:14
  47.7 11.2 %collective-permute-done.4.refs_6_ = bf16[64,2048]{1,0:T(8,128)(2,1)S(1)} collective-permute-done((bf16[64,2048]{1,0:T(8,128)(2,1)}, bf16[64,2048]{1,0:T(8,128)(2,1)S(1)}, u32[]{:S(2)}, u32[]{:S(2)}) %collective-permute-start.4) | collective-permute-done | bytes 262176 | tf_op jit(solution)/shard_map/ppermute | solution.py:14
  59.0 16.3 %collective-permute-done.5.refs_7_ = bf16[64,2048]{1,0:T(8,128)(2,1)S(1)} collective-permute-done((bf16[64,2048]{1,0:T(8,128)(2,1)}, bf16[64,2048]{1,0:T(8,128)(2,1)S(1)}, u32[]{:S(2)}, u32[]{:S(2)}) %collective-permute-start.5) | collective-permute-done | bytes 262176 | tf_op jit(solution)/shard_map/ppermute | solution.py:14
  80.0 5.3 %convolution_convert_fusion.1 = bf16[512,1024]{1,0:T(8,128)(2,1)S(1)} fusion(bf16[512,2048]{1,0:T(8,128)(2,1)S(1)} %constant_dynamic-update-slice_fusion.14.refs_0_, bf16[2048,1024]{1,0:T(8,128)(2,1)} %all-gather.7.cloned.1.call-done), kind=kOutput, calls=%fused_computation.47 | convolution fusion | flops 2148007936 | bytes 7340032 | tf_op jit(solution)/shard_map/dot_general | solution.py:26
  88.1 13.0 %collective-permute-done.7.refs_3_ = bf16[256,2048]{1,0:T(8,128)(2,1)} collective-permute-done((bf16[256,2048]{1,0:T(8,128)(2,1)}, bf16[256,2048]{1,0:T(8,128)(2,1)}, u32[]{:S(2)}, u32[]{:S(2)}) %collective-permute-start.7) | collective-permute-done | bytes 1048608 | tf_op jit(solution)/shard_map/ppermute | solution.py:14
  101.1 8.2 %collective-permute-done.8.refs_5_ = bf16[512,1024]{1,0:T(8,128)(2,1)} collective-permute-done((bf16[512,1024]{1,0:T(8,128)(2,1)S(1)}, bf16[512,1024]{1,0:T(8,128)(2,1)}, u32[]{:S(2)}, u32[]{:S(2)}) %collective-permute-start.8) | collective-permute-done | bytes 1048608 | tf_op jit(solution)/shard_map/ppermute | solution.py:14
  109.3 5.7 %add_convert_fusion.1 = bf16[512,1024]{1,0:T(8,128)(2,1)S(1)} fusion(bf16[512,1024]{1,0:T(8,128)(2,1)} %get-tuple-element.78, bf16[512,2048]{1,0:T(8,128)(2,1)} %copy-done.30, bf16[2048,1024]{1,0:T(8,128)(2,1)} %all-gather.7.cloned.1.call-done), kind=kOutput, calls=%fused_computation.39 | convolution fusion | flops 2149056512 | bytes 8388608 | tf_op jit(solution)/shard_map/dot_general | solution.py:26
  118.1 7.1 %all-gather.9.cloned.1.call-done = bf16[2048,1024]{1,0:T(8,128)(2,1)} async-done(((bf16[256,1024]{1,0:T(8,128)(2,1)}), bf16[2048,1024]{1,0:T(8,128)(2,1)}) %all-gather.9.cloned.1.call-update) | async-done | bytes 4194320 | tf_op jit(solution)/shard_map/all_gather | solution.py:88
  125.3 6.1 %convolution_convert_fusion = bf16[512,1024]{1,0:T(8,128)(2,1)} fusion(bf16[512,2048]{1,0:T(8,128)(2,1)} %get-tuple-element.84, bf16[2048,1024]{1,0:T(8,128)(2,1)} %all-gather.9.cloned.1.call-done), kind=kOutput, calls=%fused_computation.46 | convolution fusion | flops 2148007936 | bytes 7340032 | tf_op jit(solution)/shard_map/dot_general | solution.py:26
  132.8 6.2 %collective-permute-done.10.refs_3_ = bf16[256,2048]{1,0:T(8,128)(2,1)} collective-permute-done((bf16[256,2048]{1,0:T(8,128)(2,1)S(1)}, bf16[256,2048]{1,0:T(8,128)(2,1)}, u32[]{:S(2)}, u32[]{:S(2)}) %collective-permute-start.10) | collective-permute-done | bytes 1048608 | tf_op jit(solution)/shard_map/ppermute | solution.py:14
  139.1 3.8 collective-permute-done.9.refs_0_
  145.3 17.0 %collective-permute-done.12.refs_4_ = bf16[512,1024]{1,0:T(8,128)(2,1)} collective-permute-done((bf16[512,1024]{1,0:T(8,128)(2,1)}, bf16[512,1024]{1,0:T(8,128)(2,1)}, u32[]{:S(2)}, u32[]{:S(2)}) %collective-permute-start.12) | collective-permute-done | bytes 1048608 | tf_op jit(solution)/shard_map/ppermute | solution.py:14
  165.4 5.5 %add_convert_fusion = bf16[512,1024]{1,0:T(8,128)(2,1)S(1)} fusion(bf16[512,1024]{1,0:T(8,128)(2,1)} %get-tuple-element.89, bf16[512,2048]{1,0:T(8,128)(2,1)} %copy-done.30, bf16[2048,1024]{1,0:T(8,128)(2,1)} %all-gather.9.cloned.1.call-done), kind=kOutput, calls=%fused_computation.38 | convolution fusion | flops 2149056512 | bytes 8388608 | tf_op jit(solution)/shard_map/dot_general | solution.py:26
  172.6 13.3 %collective-permute-done.13.refs_1_ = bf16[256,2048]{1,0:T(8,128)(2,1)S(1)} collective-permute-done((bf16[256,2048]{1,0:T(8,128)(2,1)}, bf16[256,2048]{1,0:T(8,128)(2,1)S(1)}, u32[]{:S(2)}, u32[]{:S(2)}) %collective-permute-start.13) | collective-permute-done | bytes 1048608 | tf_op jit(solution)/shard_map/ppermute | solution.py:14
  186.9 4.4 %broadcast_in_dim.6 = bf16[1024,4096]{1,0:T(8,128)(2,1)} broadcast(bf16[]{:T(256)} %constant.249.clone.1), dimensions={} | broadcast | bytes 8388610 | tf_op jit(solution)/shard_map/broadcast_in_dim | solution.py:149
  203.0 5.8 %fusion.70 = bf16[512,512]{1,0:T(8,128)(2,1)S(1)} fusion(bf16[4096,512]{1,0:T(8,128)(2,1)} %all-gather.11.cloned.1.call-done, bf16[1024,4096]{1,0:T(8,128)(2,1)} %constant_dynamic-update-slice_fusion.16), kind=kOutput, calls=%fused_computation.59 | convolution fusion | flops 2147745792 | bytes 8912896 | tf_op jit(solution)/shard_map/dot_general | solution.py:26
  211.1 4.8 %copy.119 = f32[512,2048]{1,0:T(8,128)} copy(f32[512,2048]{1,0:T(8,128)} %param.5) | data formatting | bytes 8388608
  218.6 6.0 %fusion.67 = f32[512,512]{1,0:T(8,128)S(1)} fusion(bf16[4096,512]{1,0:T(8,128)(2,1)} %all-gather.11.cloned.1.call-done, bf16[1024,4096]{1,0:T(8,128)(2,1)} %constant_dynamic-update-slice_fusion.16, bf16[512,512]{1,0:T(8,128)(2,1)S(1)} %collective-permute-done.14, f32[512,2048]{1,0:T(8,128)} %param.5), kind=kOutput, calls=%fused_computation.58 | convolution fusion | flops 2148532224 | bytes 11010048 | tf_op jit(solution)/shard_map/dot_general | solution.py:26
  230.8 4.1 %collective-permute-done.15.refs_2_ = bf16[512,512]{1,0:T(8,128)(2,1)S(1)} collective-permute-done((bf16[512,512]{1,0:T(8,128)(2,1)S(1)}, bf16[512,512]{1,0:T(8,128)(2,1)S(1)}, u32[]{:S(2)}, u32[]{:S(2)}) %collective-permute-start.15) | collective-permute-done | bytes 524320 | tf_op jit(solution)/shard_map/ppermute | solution.py:14
  235.8 6.8 %fusion.73 = bf16[512,512]{1,0:T(8,128)(2,1)} fusion(bf16[4096,512]{1,0:T(8,128)(2,1)} %get-tuple-element.93, bf16[1024,4096]{1,0:T(8,128)(2,1)} %constant_dynamic-update-slice_fusion.16), kind=kOutput, calls=%fused_computation.60 | convolution fusion | flops 2147745792 | bytes 8912896 | tf_op jit(solution)/shard_map/dot_general | solution.py:26
  252.7 7.3 %fusion.108 = (bf16[512,512]{1,0:T(8,128)(2,1)S(1)}, f32[512,2048]{1,0:T(8,128)}) fusion(f32[512,2048]{1,0:T(8,128)} %get-tuple-element.149, bf16[512,512]{1,0:T(8,128)(2,1)} %copy-done.57, bf16[4096,512]{1,0:T(8,128)(2,1)} %get-tuple-element.93, bf16[1024,4096]{1,0:T(8,128)(2,1)} %constant_dynamic-update-slice_fusion.16, f32[512,2048]{1,0:T(8,128)} %param.5), kind=kOutput, calls=%fused_computation.131 | convolution fusion | flops 2148794368 | bytes 11534336 | tf_op jit(solution)/shard_map/dot_general | solution.py:26
  264.3 6.7 %collective-permute-start.20 = (bf16[128,512]{1,0:T(8,128)(2,1)S(1)}, bf16[128,512]{1,0:T(8,128)(2,1)S(1)}, u32[]{:S(2)}, u32[]{:S(2)}) collective-permute-start(bf16[128,512]{1,0:T(8,128)(2,1)S(1)} %get-tuple-element.162), channel_id=1, source_target_pairs={{0,24},{8,0},{16,8},{24,16},{1,25},{9,1},{17,9},{25,17},{2,26},{10... | collective-permute-start | bytes 393224 | tf_op jit(solution)/shard_map/ppermute | solution.py:14
  276.5 10.1 %collective-permute-done.21 = bf16[128,512]{1,0:T(8,128)(2,1)S(1)} collective-permute-done((bf16[128,512]{1,0:T(8,128)(2,1)S(1)}, bf16[128,512]{1,0:T(8,128)(2,1)S(1)}, u32[]{:S(2)}, u32[]{:S(2)}) %collective-permute-start.21) | collective-permute-done | bytes 131104 | tf_op jit(solution)/shard_map/ppermute | solution.py:14
  287.3 7.3 %fusion.49 = bf16[512,640]{1,0:T(8,128)(2,1)S(1)} fusion(bf16[4096,640]{1,0:T(8,128)(2,1)} %get-tuple-element.101, bf16[1024,4096]{1,0:T(8,128)(2,1)} %constant_dynamic-update-slice_fusion.16), kind=kOutput, calls=%fused_computation.51 | convolution fusion | flops 2684682240 | bytes 10092544 | tf_op jit(solution)/shard_map/dot_general | solution.py:26
  297.4 13.1 %collective-permute-done.23 = bf16[512,640]{1,0:T(8,128)(2,1)S(1)} collective-permute-done((bf16[512,640]{1,0:T(8,128)(2,1)S(1)}, bf16[512,640]{1,0:T(8,128)(2,1)S(1)}, u32[]{:S(2)}, u32[]{:S(2)}) %collective-permute-start.23) | collective-permute-done | bytes 655392 | tf_op jit(solution)/shard_map/ppermute | solution.py:14
  310.5 7.2 %fusion.107 = (bf16[512,640]{1,0:T(8,128)(2,1)S(1)}, f32[512,2048]{1,0:T(8,128)}) fusion(f32[512,2048]{1,0:T(8,128)} %get-tuple-element.147, bf16[512,640]{1,0:T(8,128)(2,1)S(1)} %collective-permute-done.23, bf16[4096,640]{1,0:T(8,128)(2,1)S(1)} %copy-done.12, bf16[1024,4096]{1,0:T(8,128)(2,1)} %constant_dynamic-update-slice_fusion.16, f32[512,2048]{1,0:T(8,128)} %param.5), kind=kOutput, calls=%fused_computation.130 | convolution fusion | flops 2685992960 | bytes 13369344 | tf_op jit(solution)/shard_map/dot_general | solution.py:26
  327.5 6.0 %collective-permute-done.27 = bf16[128,512]{1,0:T(8,128)(2,1)S(1)} collective-permute-done((bf16[128,512]{1,0:T(8,128)(2,1)S(1)}, bf16[128,512]{1,0:T(8,128)(2,1)S(1)}, u32[]{:S(2)}, u32[]{:S(2)}) %collective-permute-start.27) | collective-permute-done | bytes 131104 | tf_op jit(solution)/shard_map/ppermute | solution.py:14
  336.7 5.6 %fusion.85 = bf16[512,384]{1,0:T(8,128)(2,1)S(1)} fusion(bf16[4096,384]{1,0:T(8,128)(2,1)} %get-tuple-element.106, bf16[1024,4096]{1,0:T(8,128)(2,1)} %constant_dynamic-update-slice_fusion.16), kind=kOutput, calls=%fused_computation.64 | convolution fusion | flops 1610809344 | bytes 7733248 | tf_op jit(solution)/shard_map/dot_general | solution.py:26
  348.7 5.2 %collective-permute-done.29 = bf16[512,384]{1,0:T(8,128)(2,1)S(1)} collective-permute-done((bf16[512,384]{1,0:T(8,128)(2,1)S(1)}, bf16[512,384]{1,0:T(8,128)(2,1)S(1)}, u32[]{:S(2)}, u32[]{:S(2)}) %collective-permute-start.29) | collective-permute-done | bytes 393248 | tf_op jit(solution)/shard_map/ppermute | solution.py:14
  353.8 5.7 %fusion.112 = (bf16[512,384]{1,0:T(8,128)(2,1)S(1)}, f32[512,2048]{1,0:T(8,128)}) fusion(f32[512,2048]{1,0:T(8,128)} %get-tuple-element.145, bf16[512,384]{1,0:T(8,128)(2,1)S(1)} %collective-permute-done.29, bf16[4096,384]{1,0:T(8,128)(2,1)S(1)} %copy-done.25, bf16[1024,4096]{1,0:T(8,128)(2,1)} %constant_dynamic-update-slice_fusion.16, f32[512,2048]{1,0:T(8,128)} %param.5), kind=kOutput, calls=%fused_computation.135 | convolution fusion | flops 1611595776 | bytes 9699328 | tf_op jit(solution)/shard_map/dot_general | solution.py:26
  362.5 7.7 %collective-permute-done.30.refs_1_ = bf16[512,384]{1,0:T(8,128)(2,1)S(1)} collective-permute-done((bf16[512,384]{1,0:T(8,128)(2,1)S(1)}, bf16[512,384]{1,0:T(8,128)(2,1)S(1)}, u32[]{:S(2)}, u32[]{:S(2)}) %collective-permute-start.30) | collective-permute-done | bytes 393248 | tf_op jit(solution)/shard_map/ppermute | solution.py:14
  382.2 6.0 %collective-permute-done.37 = bf16[128,384]{1,0:T(8,128)(2,1)S(1)} collective-permute-done((bf16[128,384]{1,0:T(8,128)(2,1)S(1)}, bf16[128,384]{1,0:T(8,128)(2,1)S(1)}, u32[]{:S(2)}, u32[]{:S(2)}) %collective-permute-start.37) | collective-permute-done | bytes 98336 | tf_op jit(solution)/shard_map/ppermute | solution.py:14
  (255 shorter events, 132.2 us)
Async XLA Ops:
  7.2 72.9 %all-gather.7.cloned.1.call-start = ((), (), s32[]{:S(2)}) async-start(), calls=%async_computation | async-start | bytes 4718592 | tf_op jit(solution)/shard_map/all_gather | solution.py:88
  9.7 115.6 %all-gather.9.cloned.1.call-start = ((), (), s32[]{:S(2)}) async-start(), calls=%async_computation.1 | async-start | bytes 4718592 | tf_op jit(solution)/shard_map/all_gather | solution.py:88
  10.1 26.2 %collective-permute-start.1 = (bf16[512,1024]{1,0:T(8,128)(2,1)S(1)}, bf16[512,1024]{1,0:T(8,128)(2,1)S(1)}, u32[]{:S(2)}, u32[]{:S(2)}) collective-permute-start(bf16[512,1024]{1,0:T(8,128)(2,1)S(1)} %pad_maximum_fusion.4.refs_1_), channel_id=1, source_target_pairs={{0,1},{1,0},{2,3},{3,2},{4,5},{5,4},{6,7},{7,6},{8,9},{9,8},{10,11... | collective-permute-start | bytes 3145736 | tf_op jit(solution)/shard_map/ppermute | solution.py:14
  14.2 24.8 %collective-permute-start = (bf16[512,1024]{1,0:T(8,128)(2,1)}, bf16[512,1024]{1,0:T(8,128)(2,1)S(1)}, u32[]{:S(2)}, u32[]{:S(2)}) collective-permute-start(bf16[512,1024]{1,0:T(8,128)(2,1)} %pad_maximum_fusion.3), channel_id=1, source_target_pairs={{0,4},{4,0},{1,5},{5,1},{2,6},{6,2},{3,7},{7,3},{8,12},{12,8},{9,1... | collective-permute-start | bytes 3145736 | tf_op jit(solution)/shard_map/ppermute | solution.py:14
  40.1 163.0 %all-gather.11.cloned.1.call-start = ((), (), s32[]{:S(2)}) async-start(), calls=%async_computation.2 | async-start | bytes 4718592 | tf_op jit(solution)/shard_map/all_gather | solution.py:88
  40.1 35.2 %collective-permute-start.2 = (bf16[256,2048]{1,0:T(8,128)(2,1)}, bf16[256,2048]{1,0:T(8,128)(2,1)S(1)}, u32[]{:S(2)}, u32[]{:S(2)}) collective-permute-start(bf16[256,2048]{1,0:T(8,128)(2,1)} %get-tuple-element.59), channel_id=1, source_target_pairs={{0,4},{4,0},{1,5},{5,1},{2,6},{6,2},{3,7},{7,3},{8,12},{12,8},{9,1... | collective-permute-start | bytes 3145736 | tf_op jit(solution)/shard_map/ppermute | solution.py:14
  41.7 33.6 %collective-permute-start.3 = (bf16[512,1024]{1,0:T(8,128)(2,1)}, bf16[512,1024]{1,0:T(8,128)(2,1)S(1)}, u32[]{:S(2)}, u32[]{:S(2)}) collective-permute-start(bf16[512,1024]{1,0:T(8,128)(2,1)} %get-tuple-element.60.refs_1_), channel_id=1, source_target_pairs={{0,1},{1,0},{2,3},{3,2},{4,5},{5,4},{6,7},{7,6},{8,9},{9,8},{10,11... | collective-permute-start | bytes 3145736 | tf_op jit(solution)/shard_map/ppermute | solution.py:14
  42.2 16.8 %collective-permute-start.4 = (bf16[64,2048]{1,0:T(8,128)(2,1)}, bf16[64,2048]{1,0:T(8,128)(2,1)S(1)}, u32[]{:S(2)}, u32[]{:S(2)}) collective-permute-start(bf16[64,2048]{1,0:T(8,128)(2,1)} %get-tuple-element.63), channel_id=1, source_target_pairs={{0,8},{8,16},{16,24},{24,0},{1,9},{9,17},{17,25},{25,1},{2,10},{10... | collective-permute-start | bytes 786440 | tf_op jit(solution)/shard_map/ppermute | solution.py:14
  43.8 31.5 %collective-permute-start.5 = (bf16[64,2048]{1,0:T(8,128)(2,1)}, bf16[64,2048]{1,0:T(8,128)(2,1)S(1)}, u32[]{:S(2)}, u32[]{:S(2)}) collective-permute-start(bf16[64,2048]{1,0:T(8,128)(2,1)} %get-tuple-element.64), channel_id=1, source_target_pairs={{0,16},{8,24},{16,0},{24,8},{1,17},{9,25},{17,1},{25,9},{2,18},{10... | collective-permute-start | bytes 786440 | tf_op jit(solution)/shard_map/ppermute | solution.py:14
  46.4 28.9 %collective-permute-start.6 = (bf16[64,2048]{1,0:T(8,128)(2,1)}, bf16[64,2048]{1,0:T(8,128)(2,1)S(1)}, u32[]{:S(2)}, u32[]{:S(2)}) collective-permute-start(bf16[64,2048]{1,0:T(8,128)(2,1)} %get-tuple-element.65), channel_id=1, source_target_pairs={{0,24},{8,0},{16,8},{24,16},{1,25},{9,1},{17,9},{25,17},{2,26},{10... | collective-permute-start | bytes 786440 | tf_op jit(solution)/shard_map/ppermute | solution.py:14
  76.8 24.4 %collective-permute-start.7 = (bf16[256,2048]{1,0:T(8,128)(2,1)}, bf16[256,2048]{1,0:T(8,128)(2,1)}, u32[]{:S(2)}, u32[]{:S(2)}) collective-permute-start(bf16[256,2048]{1,0:T(8,128)(2,1)} %get-tuple-element.69.refs_2_), channel_id=1, source_target_pairs={{0,1},{1,0},{2,3},{3,2},{4,5},{5,4},{6,7},{7,6},{8,9},{9,8},{10,11... | collective-permute-start | bytes 3145736 | tf_op jit(solution)/shard_map/ppermute | solution.py:14
  85.4 23.9 %collective-permute-start.8 = (bf16[512,1024]{1,0:T(8,128)(2,1)S(1)}, bf16[512,1024]{1,0:T(8,128)(2,1)}, u32[]{:S(2)}, u32[]{:S(2)}) collective-permute-start(bf16[512,1024]{1,0:T(8,128)(2,1)S(1)} %convolution_convert_fusion.1), channel_id=1, source_target_pairs={{0,4},{4,0},{1,5},{5,1},{2,6},{6,2},{3,7},{7,3},{8,12},{12,8},{9,1... | collective-permute-start | bytes 3145736 | tf_op jit(solution)/shard_map/ppermute | solution.py:14
  116.1 118.9 %all-gather.13.cloned.1.call-start = ((), (), s32[]{:S(2)}) async-start(), calls=%async_computation.3 | async-start | bytes 4718592 | tf_op jit(solution)/shard_map/all_gather | solution.py:88
  116.1 22.9 %collective-permute-start.10 = (bf16[256,2048]{1,0:T(8,128)(2,1)S(1)}, bf16[256,2048]{1,0:T(8,128)(2,1)}, u32[]{:S(2)}, u32[]{:S(2)}) collective-permute-start(bf16[256,2048]{1,0:T(8,128)(2,1)S(1)} %copy-done.1), channel_id=1, source_target_pairs={{0,1},{1,0},{2,3},{3,2},{4,5},{5,4},{6,7},{7,6},{8,9},{9,8},{10,11... | collective-permute-start | bytes 3145736 | tf_op jit(solution)/shard_map/ppermute | solution.py:14
  116.8 26.1 %collective-permute-start.9 = (bf16[256,2048]{1,0:T(8,128)(2,1)S(1)}, bf16[256,2048]{1,0:T(8,128)(2,1)S(1)}, u32[]{:S(2)}, u32[]{:S(2)}) collective-permute-start(bf16[256,2048]{1,0:T(8,128)(2,1)S(1)} %copy-done.10), channel_id=1, source_target_pairs={{0,4},{4,0},{1,5},{5,1},{2,6},{6,2},{3,7},{7,3},{8,12},{12,8},{9,1... | collective-permute-start | bytes 3145736 | tf_op jit(solution)/shard_map/ppermute | solution.py:14
  131.4 30.9 %collective-permute-start.12 = (bf16[512,1024]{1,0:T(8,128)(2,1)}, bf16[512,1024]{1,0:T(8,128)(2,1)}, u32[]{:S(2)}, u32[]{:S(2)}) collective-permute-start(bf16[512,1024]{1,0:T(8,128)(2,1)} %convolution_convert_fusion), channel_id=1, source_target_pairs={{0,4},{4,0},{1,5},{5,1},{2,6},{6,2},{3,7},{7,3},{8,12},{12,8},{9,1... | collective-permute-start | bytes 3145736 | tf_op jit(solution)/shard_map/ppermute | solution.py:14
  143.9 19.1 %collective-permute-start.11 = (bf16[256,2048]{1,0:T(8,128)(2,1)}, bf16[256,2048]{1,0:T(8,128)(2,1)S(1)}, u32[]{:S(2)}, u32[]{:S(2)}) collective-permute-start(bf16[256,2048]{1,0:T(8,128)(2,1)} %get-tuple-element.81.refs_0_), channel_id=1, source_target_pairs={{0,1},{1,0},{2,3},{3,2},{4,5},{5,4},{6,7},{7,6},{8,9},{9,8},{10,11... | collective-permute-start | bytes 3145736 | tf_op jit(solution)/shard_map/ppermute | solution.py:14
  164.1 123.2 %all-gather.15.cloned.1.call-start = ((), (), s32[]{:S(2)}) async-start(), calls=%async_computation.4 | async-start | bytes 5898240 | tf_op jit(solution)/shard_map/all_gather | solution.py:88
  164.3 21.6 %collective-permute-start.13 = (bf16[256,2048]{1,0:T(8,128)(2,1)}, bf16[256,2048]{1,0:T(8,128)(2,1)S(1)}, u32[]{:S(2)}, u32[]{:S(2)}) collective-permute-start(bf16[256,2048]{1,0:T(8,128)(2,1)} %get-tuple-element.88.refs_0_), channel_id=1, source_target_pairs={{0,1},{1,0},{2,3},{3,2},{4,5},{5,4},{6,7},{7,6},{8,9},{9,8},{10,11... | collective-permute-start | bytes 3145736 | tf_op jit(solution)/shard_map/ppermute | solution.py:14
  186.9 147.5 %all-gather.17.cloned.1.call-start = ((), (), s32[]{:S(2)}) async-start(), calls=%async_computation.5 | async-start | bytes 3538944 | tf_op jit(solution)/shard_map/all_gather | solution.py:88
  229.7 19.7 %collective-permute-start.18 = (bf16[256,2048]{1,0:T(8,128)(2,1)}, bf16[256,2048]{1,0:T(8,128)(2,1)}, u32[]{:S(2)}, u32[]{:S(2)}) collective-permute-start(bf16[256,2048]{1,0:T(8,128)(2,1)} %constant_dynamic-update-slice_fusion), channel_id=1, source_target_pairs={{0,1},{1,0},{2,3},{3,2},{4,5},{5,4},{6,7},{7,6},{8,9},{9,8},{10,11... | collective-permute-start | bytes 3145736 | tf_op jit(solution)/shard_map/ppermute | solution.py:14
  245.4 16.4 %collective-permute-start.19 = (bf16[1024,512]{1,0:T(8,128)(2,1)}, bf16[1024,512]{1,0:T(8,128)(2,1)}, u32[]{:S(2)}, u32[]{:S(2)}) collective-permute-start(bf16[1024,512]{1,0:T(8,128)(2,1)} %pad_maximum_fusion.5), channel_id=1, source_target_pairs={{0,2},{2,0},{1,3},{3,1},{4,6},{6,4},{5,7},{7,5},{8,10},{10,8},{9,1... | collective-permute-start | bytes 3145736 | tf_op jit(solution)/shard_map/ppermute | solution.py:14
  260.0 27.3 %collective-permute-start.17 = (bf16[512,512]{1,0:T(8,128)(2,1)S(1)}, bf16[512,512]{1,0:T(8,128)(2,1)}, u32[]{:S(2)}, u32[]{:S(2)}) collective-permute-start(bf16[512,512]{1,0:T(8,128)(2,1)S(1)} %get-tuple-element.146.refs_1_), channel_id=1, source_target_pairs={{0,4},{4,0},{1,5},{5,1},{2,6},{6,2},{3,7},{7,3},{8,12},{12,8},{9,1... | collective-permute-start | bytes 1572872 | tf_op jit(solution)/shard_map/ppermute | solution.py:14
  264.3 12.2 %collective-permute-start.20 = (bf16[128,512]{1,0:T(8,128)(2,1)S(1)}, bf16[128,512]{1,0:T(8,128)(2,1)S(1)}, u32[]{:S(2)}, u32[]{:S(2)}) collective-permute-start(bf16[128,512]{1,0:T(8,128)(2,1)S(1)} %get-tuple-element.162), channel_id=1, source_target_pairs={{0,24},{8,0},{16,8},{24,16},{1,25},{9,1},{17,9},{25,17},{2,26},{10... | collective-permute-start | bytes 393224 | tf_op jit(solution)/shard_map/ppermute | solution.py:14
  271.0 15.6 %collective-permute-start.21 = (bf16[128,512]{1,0:T(8,128)(2,1)S(1)}, bf16[128,512]{1,0:T(8,128)(2,1)S(1)}, u32[]{:S(2)}, u32[]{:S(2)}) collective-permute-start(bf16[128,512]{1,0:T(8,128)(2,1)S(1)} %get-tuple-element.164), channel_id=1, source_target_pairs={{0,16},{8,24},{16,0},{24,8},{1,17},{9,25},{17,1},{25,9},{2,18},{10... | collective-permute-start | bytes 393224 | tf_op jit(solution)/shard_map/ppermute | solution.py:14
  274.0 12.6 %collective-permute-start.22 = (bf16[128,512]{1,0:T(8,128)(2,1)S(1)}, bf16[128,512]{1,0:T(8,128)(2,1)S(1)}, u32[]{:S(2)}, u32[]{:S(2)}) collective-permute-start(bf16[128,512]{1,0:T(8,128)(2,1)S(1)} %get-tuple-element.163), channel_id=1, source_target_pairs={{0,8},{8,16},{16,24},{24,0},{1,9},{9,17},{17,25},{25,1},{2,10},{10... | collective-permute-start | bytes 393224 | tf_op jit(solution)/shard_map/ppermute | solution.py:14
  294.6 15.8 %collective-permute-start.23 = (bf16[512,640]{1,0:T(8,128)(2,1)S(1)}, bf16[512,640]{1,0:T(8,128)(2,1)S(1)}, u32[]{:S(2)}, u32[]{:S(2)}) collective-permute-start(bf16[512,640]{1,0:T(8,128)(2,1)S(1)} %fusion.49), channel_id=1, source_target_pairs={{0,4},{4,0},{1,5},{5,1},{2,6},{6,2},{3,7},{7,3},{8,12},{12,8},{9,1... | collective-permute-start | bytes 1966088 | tf_op jit(solution)/shard_map/ppermute | solution.py:14
  297.3 21.9 %collective-permute-start.25 = (bf16[1024,512]{1,0:T(8,128)(2,1)S(1)}, bf16[1024,512]{1,0:T(8,128)(2,1)S(1)}, u32[]{:S(2)}, u32[]{:S(2)}) collective-permute-start(bf16[1024,512]{1,0:T(8,128)(2,1)S(1)} %pad_maximum_fusion.6), channel_id=1, source_target_pairs={{0,2},{2,0},{1,3},{3,1},{4,6},{6,4},{5,7},{7,5},{8,10},{10,8},{9,1... | collective-permute-start | bytes 3145736 | tf_op jit(solution)/shard_map/ppermute | solution.py:14
  317.6 16.7 %collective-permute-start.24 = (bf16[512,640]{1,0:T(8,128)(2,1)S(1)}, bf16[512,640]{1,0:T(8,128)(2,1)S(1)}, u32[]{:S(2)}, u32[]{:S(2)}) collective-permute-start(bf16[512,640]{1,0:T(8,128)(2,1)S(1)} %get-tuple-element.144.refs_1_), channel_id=1, source_target_pairs={{0,4},{4,0},{1,5},{5,1},{2,6},{6,2},{3,7},{7,3},{8,12},{12,8},{9,1... | collective-permute-start | bytes 1966088 | tf_op jit(solution)/shard_map/ppermute | solution.py:14
  345.7 15.3 %collective-permute-start.32 = (bf16[128,640]{1,0:T(8,128)(2,1)S(1)}, bf16[128,640]{1,0:T(8,128)(2,1)S(1)}, u32[]{:S(2)}, u32[]{:S(2)}) collective-permute-start(bf16[128,640]{1,0:T(8,128)(2,1)S(1)} %get-tuple-element.156), channel_id=1, source_target_pairs={{0,24},{8,0},{16,8},{24,16},{1,25},{9,1},{17,9},{25,17},{2,26},{10... | collective-permute-start | bytes 491528 | tf_op jit(solution)/shard_map/ppermute | solution.py:14
  345.8 16.0 %collective-permute-start.33 = (bf16[128,640]{1,0:T(8,128)(2,1)S(1)}, bf16[128,640]{1,0:T(8,128)(2,1)S(1)}, u32[]{:S(2)}, u32[]{:S(2)}) collective-permute-start(bf16[128,640]{1,0:T(8,128)(2,1)S(1)} %get-tuple-element.158), channel_id=1, source_target_pairs={{0,16},{8,24},{16,0},{24,8},{1,17},{9,25},{17,1},{25,9},{2,18},{10... | collective-permute-start | bytes 491528 | tf_op jit(solution)/shard_map/ppermute | solution.py:14
  346.7 15.0 %collective-permute-start.34 = (bf16[128,640]{1,0:T(8,128)(2,1)S(1)}, bf16[128,640]{1,0:T(8,128)(2,1)S(1)}, u32[]{:S(2)}, u32[]{:S(2)}) collective-permute-start(bf16[128,640]{1,0:T(8,128)(2,1)S(1)} %get-tuple-element.157), channel_id=1, source_target_pairs={{0,8},{8,16},{16,24},{24,0},{1,9},{9,17},{17,25},{25,1},{2,10},{10... | collective-permute-start | bytes 491528 | tf_op jit(solution)/shard_map/ppermute | solution.py:14
  (71 other events, 436.2 us)
Sparse Core Ops, SparseCore 0:
  10.2 67.4 all-gather.6
  79.2 45.9 all-gather.8
  126.9 45.8 all-gather.10
  174.8 45.8 all-gather.12
  222.2 58.0 all-gather.14
  281.8 42.3 all-gather.16
